TPU v7x, 32 devices: a whole 2x2x4 slice. The times are simulated.
32 devices in a mesh: seq: 8 (over z, x), tp: 4 (over y, core).
Axes of the slice: x: 2, y: 2, z: 4, core: 2. Of those that a mesh axis runs over, the one named last changes fastest.
Arguments:
- source: bfloat16 [8192, 1024], P('seq'), may hold values from -6 to 6
- target: bfloat16 [4096, 1024], P('seq'), may hold values from -6 to 6
- source_document: int32 [8192], replicated, may hold values from -1 to 16, as said below
- target_document: int32 [4096], replicated, may hold values from -1 to 16, as said below
- cotangent: bfloat16 [4096, 1024], P('seq'), may hold values from -6 to 6
- encoder_attention: bfloat16 [3, 1024, 1024], P(None, None, 'tp'), may hold values from -0.1875 to 0.1875
- encoder_mixing: bfloat16 [1024, 1024], P('tp'), may hold values from -1 to 1
- encoder_gains: float32 [2, 1024], replicated, may hold values from 0.1 to 1.9
- encoder_inner: bfloat16 [1024, 4096], P(None, 'tp'), may hold values from -0.1875 to 0.1875
- encoder_outer: bfloat16 [4096, 1024], P('tp'), may hold values from -0.09375 to 0.09375
- encoder_prefix: bfloat16 [2, 30, 1024], P(None, None, 'tp'), may hold values from -6 to 6
- encoder_down: bfloat16 [1024, 512], P(None, 'tp'), may hold values from -0.1875 to 0.1875
- encoder_up: bfloat16 [512, 1024], P('tp'), may hold values from -0.25 to 0.25
- decoder_attention: bfloat16 [3, 1024, 1024], P(None, None, 'tp'), may hold values from -0.1875 to 0.1875
- decoder_mixing: bfloat16 [1024, 1024], P('tp'), may hold values from -1 to 1
- decoder_prefix: bfloat16 [2, 30, 1024], P(None, None, 'tp'), may hold values from -6 to 6
- cross_query: bfloat16 [1024, 1024], P(None, 'tp'), may hold values from -0.1875 to 0.1875
- cross_memory: bfloat16 [2, 1024, 1024], P(None, None, 'tp'), may hold values from -0.1875 to 0.1875
- cross_mixing: bfloat16 [1024, 1024], P('tp'), may hold values from -1 to 1
- cross_prefix: bfloat16 [2, 30, 1024], P(None, None, 'tp'), may hold values from -6 to 6
- decoder_gains: float32 [3, 1024], replicated, may hold values from 0.1 to 1.9
- decoder_inner: bfloat16 [1024, 4096], P(None, 'tp'), may hold values from -0.1875 to 0.1875
- decoder_outer: bfloat16 [4096, 1024], P('tp'), may hold values from -0.09375 to 0.09375
- decoder_down: bfloat16 [1024, 512], P(None, 'tp'), may hold values from -0.1875 to 0.1875
- decoder_up: bfloat16 [512, 1024], P('tp'), may hold values from -0.25 to 0.25
Outputs:
- decoded: float32 [4096, 1024], P('seq')
- source_gradient: float32 [8192, 1024], P('seq')
- target_gradient: float32 [4096, 1024], P('seq')
- encoder_prefix_gradient: float32 [2, 30, 1024], P(None, None, 'tp')
- encoder_down_gradient: float32 [1024, 512], P(None, 'tp')
- encoder_up_gradient: float32 [512, 1024], P('tp')
- decoder_prefix_gradient: float32 [2, 30, 1024], P(None, None, 'tp')
- cross_prefix_gradient: float32 [2, 30, 1024], P(None, None, 'tp')
- decoder_down_gradient: float32 [1024, 512], P(None, 'tp')
- decoder_up_gradient: float32 [512, 1024], P('tp')
Inputs may be any that keep to these rules, and one draw needn't show every extreme that they name: Document numbers never fall along the stream, apart from padding; a number names the same document in source_document and target_document, and every document has real slots in both. The slots of one document, in either stream, lie on one index of seq or on two neighbouring ones, the same indices in both streams, and number at most 1024 source and 512 target slots, which some document reaches in every draw; every index but the first begins with a document that began on the index before. Padding slots stand only at the end of a document. `target_document`: as for source_document.
All inputs are finite; a program needn't handle non-finite values.
Results may differ from a plain program's by a relative error of at most 0.03.
Values may be sent and summed in bfloat16 or wider, within the bound.
A program may use at most 256 MiB of HBM per device.

v0:
```python
from functools import partial
import math

import jax
import jax.numpy as jnp
from jax import lax
from jax.sharding import PartitionSpec as P

HEAD_DIM = 64


EPSILON = 1e-05
NEGATIVE = -1e30


def extended(x, sides, width):
    for axis, dim in sides:
        size, length = (lax.axis_size(axis), x.shape[dim])
        up = [(i, (i + 1) % size) for i in range(size - 1)]
        down = [(j, i) for i, j in up]
        last = lax.slice_in_dim(x, length - width, length, axis=dim)
        initial = lax.slice_in_dim(x, 0, width, axis=dim)
        before = lax.ppermute(last, axis, up)
        after = lax.ppermute(initial, axis, down)
        x = jnp.concatenate([before, x, after], axis=dim)
    return x


def normalize(inputs, scaling):
    centered = inputs - jnp.mean(inputs, axis=-1, keepdims=True)
    spread = lax.rsqrt(jnp.mean(centered * centered, axis=-1, keepdims=True) + EPSILON)
    return scaling * (centered * spread)


def normalize_back(inputs, scaling, gradient):
    _, pullback = jax.vjp(partial(normalize, scaling=scaling), inputs)
    return pullback(gradient)[0]


def exact_gelu(inputs):
    return jax.nn.gelu(inputs, approximate=False)


def gelu_back(inputs, gradient):
    _, pullback = jax.vjp(exact_gelu, inputs)
    return pullback(gradient)[0]


def as_heads(matrix):
    return matrix.reshape(matrix.shape[0], matrix.shape[1] // HEAD_DIM, HEAD_DIM)


def own_docs(docs_all, rows):
    return lax.dynamic_slice_in_dim(docs_all, lax.axis_index("seq") * rows, rows)


def window_docs(docs_all, rows):
    filler = jnp.full((rows,), -1, jnp.int32)
    padded = jnp.concatenate([filler, docs_all, filler])
    return lax.dynamic_slice_in_dim(padded, lax.axis_index("seq") * rows, 3 * rows)


def prefix_scores(queries, prefix_keys):
    return jnp.einsum(
        "qhd,phd->hqp", queries, prefix_keys, preferred_element_type=jnp.float32
    ) * HEAD_DIM ** (-0.5)


def window_scores(queries, key_heads, key_doc, key_places, query_doc, query_places, causal):
    raw_scores = jnp.einsum(
        "qhd,khd->hqk", queries, key_heads, preferred_element_type=jnp.float32
    ) * HEAD_DIM ** (-0.5)
    allowed = (key_doc[None, :] == query_doc[:, None]) & (key_doc[None, :] >= 0)
    if causal:
        allowed = allowed & (key_places[None, :] <= query_places[:, None])
    return jnp.where(allowed[None], raw_scores, NEGATIVE)


def stacked(array, block):
    return array.reshape((array.shape[0] // block, block) + array.shape[1:])


def attend(query_in, key_in, weights, prefix, query_doc, key_doc, query_places, key_places, causal):
    query_weight, key_weight, value_weight, mixing_weight = weights
    queries = jnp.dot(query_in, query_weight, preferred_element_type=jnp.float32).astype(
        jnp.bfloat16
    )
    rows = key_in.shape[0]
    own_rows = jnp.stack(
        [
            jnp.dot(key_in, key_weight, preferred_element_type=jnp.float32).astype(jnp.bfloat16),
            jnp.dot(key_in, value_weight, preferred_element_type=jnp.float32).astype(jnp.bfloat16),
        ],
        axis=1,
    )
    window = extended(own_rows, (("seq", 0),), rows)
    key_heads = as_heads(window[:, 0])
    value_heads = as_heads(window[:, 1])
    query_heads = as_heads(queries)
    prefix_keys = as_heads(prefix[0])
    prefix_values = as_heads(prefix[1])
    query_rows = query_heads.shape[0]
    block = math.gcd(query_rows, 512)

    def forward_block(inputs):
        block_queries, block_doc, block_places = inputs
        opening = prefix_scores(block_queries, prefix_keys)
        main = window_scores(
            block_queries, key_heads, key_doc, key_places, block_doc, block_places, causal
        )
        highest = jnp.maximum(jnp.max(opening, axis=2), jnp.max(main, axis=2))
        summed = jnp.sum(jnp.exp(opening - highest[:, :, None]), axis=2) + jnp.sum(
            jnp.exp(main - highest[:, :, None]), axis=2
        )
        log_total = highest + jnp.log(summed)
        open_chances = jnp.exp(opening - log_total[:, :, None]).astype(jnp.bfloat16)
        main_chances = jnp.exp(main - log_total[:, :, None]).astype(jnp.bfloat16)
        blended = jnp.einsum(
            "hqp,phd->qhd", open_chances, prefix_values, preferred_element_type=jnp.float32
        )
        blended = blended + jnp.einsum(
            "hqk,khd->qhd", main_chances, value_heads, preferred_element_type=jnp.float32
        )
        return (blended.reshape(block, -1), log_total)

    attended, log_total = lax.map(
        forward_block,
        (stacked(query_heads, block), stacked(query_doc, block), stacked(query_places, block)),
    )
    attended = attended.reshape(query_rows, -1)
    branch_piece = jnp.dot(
        attended.astype(jnp.bfloat16), mixing_weight, preferred_element_type=jnp.float32
    )
    saved = (queries, window, log_total, attended)
    return (branch_piece, saved)


def attend_back(
    gradient, weights, prefix, query_doc, key_doc, query_places, key_places, causal, saved
):
    query_weight, key_weight, value_weight, mixing_weight = weights
    queries, window, log_total, attended = saved
    temper = HEAD_DIM ** (-0.5)
    key_heads = as_heads(window[:, 0])
    value_heads = as_heads(window[:, 1])
    query_heads = as_heads(queries)
    prefix_keys = as_heads(prefix[0])
    prefix_values = as_heads(prefix[1])
    query_rows = query_heads.shape[0]
    block = math.gcd(query_rows, 512)
    grad_attended = jnp.einsum(
        "qe,ce->qc",
        gradient.astype(jnp.bfloat16),
        mixing_weight,
        preferred_element_type=jnp.float32,
    ).astype(jnp.bfloat16)
    grad_heads = as_heads(grad_attended)

    def backward_block(carried, inputs):
        key_sum, value_sum, prefix_key_sum, prefix_value_sum = carried
        block_queries, block_grad, block_attended, block_doc, block_places, block_total = inputs
        offsets = jnp.sum(block_grad.astype(jnp.float32) * block_attended, axis=2).T
        opening = prefix_scores(block_queries, prefix_keys)
        open_chances = jnp.exp(opening - block_total[:, :, None])
        open_grad = jnp.einsum(
            "qhd,phd->hqp", block_grad, prefix_values, preferred_element_type=jnp.float32
        )
        grad_opening = (open_chances * (open_grad - offsets[:, :, None])).astype(jnp.bfloat16)
        main = window_scores(
            block_queries, key_heads, key_doc, key_places, block_doc, block_places, causal
        )
        main_chances = jnp.exp(main - block_total[:, :, None])
        main_grad = jnp.einsum(
            "qhd,khd->hqk", block_grad, value_heads, preferred_element_type=jnp.float32
        )
        grad_main = (main_chances * (main_grad - offsets[:, :, None])).astype(jnp.bfloat16)
        grad_query = jnp.einsum(
            "hqp,phd->qhd", grad_opening, prefix_keys, preferred_element_type=jnp.float32
        )
        grad_query = (
            grad_query
            + jnp.einsum("hqk,khd->qhd", grad_main, key_heads, preferred_element_type=jnp.float32)
        ) * temper
        key_sum = (
            key_sum
            + jnp.einsum(
                "hqk,qhd->khd", grad_main, block_queries, preferred_element_type=jnp.float32
            )
            * temper
        )
        value_sum = value_sum + jnp.einsum(
            "hqk,qhd->khd",
            main_chances.astype(jnp.bfloat16),
            block_grad,
            preferred_element_type=jnp.float32,
        )
        prefix_key_sum = (
            prefix_key_sum
            + jnp.einsum(
                "hqp,qhd->phd", grad_opening, block_queries, preferred_element_type=jnp.float32
            )
            * temper
        )
        prefix_value_sum = prefix_value_sum + jnp.einsum(
            "hqp,qhd->phd",
            open_chances.astype(jnp.bfloat16),
            block_grad,
            preferred_element_type=jnp.float32,
        )
        return (
            (key_sum, value_sum, prefix_key_sum, prefix_value_sum),
            grad_query.reshape(block, -1),
        )

    initial = (
        jnp.zeros(key_heads.shape, jnp.float32),
        jnp.zeros(value_heads.shape, jnp.float32),
        jnp.zeros(prefix_keys.shape, jnp.float32),
        jnp.zeros(prefix_values.shape, jnp.float32),
    )
    inputs = (
        stacked(query_heads, block),
        stacked(grad_heads, block),
        stacked(as_heads(attended), block),
        stacked(query_doc, block),
        stacked(query_places, block),
        log_total,
    )
    (key_sum, value_sum, prefix_key_grad, prefix_value_grad), grad_queries = lax.scan(
        backward_block, initial, inputs
    )
    grad_queries = grad_queries.reshape(query_rows, -1)
    rows = key_sum.shape[0] // 3
    terms = jnp.stack([key_sum.reshape(3 * rows, -1), value_sum.reshape(3 * rows, -1)], axis=1)
    outward = jnp.concatenate([terms[:rows], terms[2 * rows :]], axis=0)
    returned = extended(outward, (("seq", 0),), rows)
    own_total = terms[rows : 2 * rows] + returned[:rows] + returned[3 * rows :]
    key_total = own_total[:, 0]
    value_total = own_total[:, 1]
    query_piece = jnp.einsum(
        "qc,ec->qe",
        grad_queries.astype(jnp.bfloat16),
        query_weight,
        preferred_element_type=jnp.float32,
    )
    key_piece = jnp.einsum(
        "kc,ec->ke", key_total.astype(jnp.bfloat16), key_weight, preferred_element_type=jnp.float32
    )
    key_piece = key_piece + jnp.einsum(
        "kc,ec->ke",
        value_total.astype(jnp.bfloat16),
        value_weight,
        preferred_element_type=jnp.float32,
    )
    prefix_grad = jnp.stack(
        [
            prefix_key_grad.reshape(prefix_key_grad.shape[0], -1),
            prefix_value_grad.reshape(prefix_value_grad.shape[0], -1),
        ]
    )
    return (query_piece, key_piece, prefix_grad)


def feed_forward(hidden, inner_weight, outer_weight, down_weight, up_weight):
    rounded = hidden.astype(jnp.bfloat16)
    inner_sum = jnp.dot(rounded, inner_weight, preferred_element_type=jnp.float32)
    side_sum = jnp.dot(rounded, down_weight, preferred_element_type=jnp.float32)
    inner_gelu = exact_gelu(inner_sum).astype(jnp.bfloat16)
    side_gelu = exact_gelu(side_sum).astype(jnp.bfloat16)
    branch_piece = jnp.dot(
        inner_gelu, outer_weight, preferred_element_type=jnp.float32
    ) + 4.0 * jnp.dot(side_gelu, up_weight, preferred_element_type=jnp.float32)
    return (branch_piece, (rounded, inner_sum, side_sum, side_gelu))


def feed_back(gradient, hidden, inner_weight, outer_weight, down_weight, up_weight):
    rounded = hidden.astype(jnp.bfloat16)
    inner_sum = jnp.dot(rounded, inner_weight, preferred_element_type=jnp.float32)
    side_sum = jnp.dot(rounded, down_weight, preferred_element_type=jnp.float32)
    side_gelu = exact_gelu(side_sum).astype(jnp.bfloat16)
    grad_low = gradient.astype(jnp.bfloat16)
    grad_four = (4.0 * gradient).astype(jnp.bfloat16)
    grad_inner = gelu_back(
        inner_sum,
        jnp.einsum("qe,fe->qf", grad_low, outer_weight, preferred_element_type=jnp.float32),
    ).astype(jnp.bfloat16)
    grad_side = gelu_back(
        side_sum, jnp.einsum("qe,ae->qa", grad_four, up_weight, preferred_element_type=jnp.float32)
    ).astype(jnp.bfloat16)
    up_grad = jnp.einsum("qa,qe->ae", side_gelu, grad_four, preferred_element_type=jnp.float32)
    down_grad = jnp.einsum("qe,qa->ea", rounded, grad_side, preferred_element_type=jnp.float32)
    hidden_piece = jnp.einsum(
        "qf,ef->qe", grad_inner, inner_weight, preferred_element_type=jnp.float32
    )
    hidden_piece = hidden_piece + jnp.einsum(
        "qa,ea->qe", grad_side, down_weight, preferred_element_type=jnp.float32
    )
    return (hidden_piece, down_grad, up_grad)


def branch_total(piece_sum):
    return lax.psum(piece_sum, "tp")


def input_total(piece_sum):
    return lax.psum(piece_sum, "tp")


def on_device(
    source,
    target,
    source_document,
    target_document,
    cotangent,
    encoder_attention,
    encoder_mixing,
    encoder_gains,
    encoder_inner,
    encoder_outer,
    encoder_prefix,
    encoder_down,
    encoder_up,
    decoder_attention,
    decoder_mixing,
    decoder_prefix,
    cross_query,
    cross_memory,
    cross_mixing,
    cross_prefix,
    decoder_gains,
    decoder_inner,
    decoder_outer,
    decoder_down,
    decoder_up,
):
    seq_index = lax.axis_index("seq")
    source_rows = source.shape[0]
    target_rows = target.shape[0]
    source_places = seq_index * source_rows + jnp.arange(source_rows, dtype=jnp.int32)
    target_places = seq_index * target_rows + jnp.arange(target_rows, dtype=jnp.int32)
    source_key_places = (seq_index - 1) * source_rows + jnp.arange(3 * source_rows, dtype=jnp.int32)
    target_key_places = (seq_index - 1) * target_rows + jnp.arange(3 * target_rows, dtype=jnp.int32)
    source_own = own_docs(source_document, source_rows)
    target_own = own_docs(target_document, target_rows)
    source_window = window_docs(source_document, source_rows)
    target_window = window_docs(target_document, target_rows)
    encoder_weights = (
        encoder_attention[0],
        encoder_attention[1],
        encoder_attention[2],
        encoder_mixing,
    )
    decoder_weights = (
        decoder_attention[0],
        decoder_attention[1],
        decoder_attention[2],
        decoder_mixing,
    )
    cross_weights = (cross_query, cross_memory[0], cross_memory[1], cross_mixing)
    encoder_piece, encoder_saved = attend(
        source,
        source,
        encoder_weights,
        encoder_prefix,
        source_own,
        source_window,
        source_places,
        source_key_places,
        False,
    )
    encoder_first = source.astype(jnp.float32) + branch_total(encoder_piece)
    encoder_middle = normalize(encoder_first, encoder_gains[0])
    encoder_feed, encoder_stored = feed_forward(
        encoder_middle, encoder_inner, encoder_outer, encoder_down, encoder_up
    )
    encoder_second = encoder_middle + branch_total(encoder_feed)
    encoded = normalize(encoder_second, encoder_gains[1])
    decoder_piece, decoder_saved = attend(
        target,
        target,
        decoder_weights,
        decoder_prefix,
        target_own,
        target_window,
        target_places,
        target_key_places,
        True,
    )
    decoder_first = target.astype(jnp.float32) + branch_total(decoder_piece)
    decoder_middle = normalize(decoder_first, decoder_gains[0])
    cross_piece, cross_saved = attend(
        decoder_middle.astype(jnp.bfloat16),
        encoded.astype(jnp.bfloat16),
        cross_weights,
        cross_prefix,
        target_own,
        source_window,
        target_places,
        source_key_places,
        False,
    )
    decoder_second = decoder_middle + branch_total(cross_piece)
    decoder_late = normalize(decoder_second, decoder_gains[1])
    decoder_feed, decoder_stored = feed_forward(
        decoder_late, decoder_inner, decoder_outer, decoder_down, decoder_up
    )
    decoder_third = decoder_late + branch_total(decoder_feed)
    real_rows = (target_own >= 0).astype(jnp.float32)[:, None]
    decoded = normalize(decoder_third, decoder_gains[2]) * real_rows
    grad_third = normalize_back(
        decoder_third, decoder_gains[2], cotangent.astype(jnp.float32) * real_rows
    )
    feed_piece, decoder_down_gradient, decoder_up_gradient = feed_back(
        grad_third, decoder_late, decoder_inner, decoder_outer, decoder_down, decoder_up
    )
    grad_late = grad_third + input_total(feed_piece)
    grad_second = normalize_back(decoder_second, decoder_gains[1], grad_late)
    query_piece, key_piece, cross_prefix_gradient = attend_back(
        grad_second,
        cross_weights,
        cross_prefix,
        target_own,
        source_window,
        target_places,
        source_key_places,
        False,
        cross_saved,
    )
    query_total, encoded_gradient = lax.psum((query_piece, key_piece), "tp")
    grad_first = normalize_back(decoder_first, decoder_gains[0], grad_second + query_total)
    query_piece, key_piece, decoder_prefix_gradient = attend_back(
        grad_first,
        decoder_weights,
        decoder_prefix,
        target_own,
        target_window,
        target_places,
        target_key_places,
        True,
        decoder_saved,
    )
    target_gradient = grad_first + input_total(query_piece + key_piece)
    encoder_grad_second = normalize_back(encoder_second, encoder_gains[1], encoded_gradient)
    feed_piece, encoder_down_gradient, encoder_up_gradient = feed_back(
        encoder_grad_second, encoder_middle, encoder_inner, encoder_outer, encoder_down, encoder_up
    )
    encoder_grad_middle = encoder_grad_second + input_total(feed_piece)
    encoder_grad_first = normalize_back(encoder_first, encoder_gains[0], encoder_grad_middle)
    query_piece, key_piece, encoder_prefix_gradient = attend_back(
        encoder_grad_first,
        encoder_weights,
        encoder_prefix,
        source_own,
        source_window,
        source_places,
        source_key_places,
        False,
        encoder_saved,
    )
    source_gradient = encoder_grad_first + input_total(query_piece + key_piece)
    weight_totals = lax.psum(
        (
            encoder_prefix_gradient,
            encoder_down_gradient,
            encoder_up_gradient,
            decoder_prefix_gradient,
            cross_prefix_gradient,
            decoder_down_gradient,
            decoder_up_gradient,
        ),
        "seq",
    )
    return (decoded, source_gradient, target_gradient) + tuple(weight_totals)


def solution(mesh):
    return jax.shard_map(
        on_device,
        mesh=mesh,
        in_specs=(
            P("seq", None),
            P("seq", None),
            P(),
            P(),
            P("seq", None),
            P(None, None, "tp"),
            P("tp", None),
            P(),
            P(None, "tp"),
            P("tp", None),
            P(None, None, "tp"),
            P(None, "tp"),
            P("tp", None),
            P(None, None, "tp"),
            P("tp", None),
            P(None, None, "tp"),
            P(None, "tp"),
            P(None, None, "tp"),
            P("tp", None),
            P(None, None, "tp"),
            P(),
            P(None, "tp"),
            P("tp", None),
            P(None, "tp"),
            P("tp", None),
        ),
        out_specs=(
            P("seq", None),
            P("seq", None),
            P("seq", None),
            P(None, None, "tp"),
            P(None, "tp"),
            P("tp", None),
            P(None, None, "tp"),
            P(None, None, "tp"),
            P(None, "tp"),
            P("tp", None),
        ),
        check_vma=False,
    )
```

profile of v0, /device:TPU:0, one launch (start us, length us, event | category | flops | bytes accessed | tf_op | source)
XLA Modules:
  0.0 1689.4 jit_solution(12368012665360869817)
XLA Ops:
  37.6 46.9 %collective-permute-done = bf16[512,2,256]{2,0,1:T(8,128)(2,1)} collective-permute-done((bf16[512,2,256]{2,0,1:T(8,128)(2,1)}, bf16[512,2,256]{2,0,1:T(8,128)(2,1)}, u32[]{:S(2)}, u32[]{:S(2)}) %collective-permute-start) | collective-permute-done | bytes 524320 | tf_op jit(solution)/shard_map/ppermute | solution.py:23
  107.2 79.9 %while.5 = (s32[]{:T(128)}, f32[2,512,256]{1,2,0:T(8,128)}, f32[2,4,512]{2,1,0:T(4,128)}, bf16[2,512,4,64]{1,3,2,0:T(8,128)(2,1)S(1)}, bf16[30,4,64]{2,0,1:T(8,1...) while((s32[]{:T(128)}, f32[2,512,256]{1,2,0:T(8,128)}, ...), condition=%wide.region_13.14_spmd, body=%wide.region_8.13_spmd.sunk | while | flops 1699193856 | bytes 103697096 | solution.py:126
  108.8 12.3 fusion.409
  122.1 12.0 exponential_reduce_fusion.9
  134.8 11.3 fusion.411
  148.5 12.3 fusion.409
  161.8 12.0 exponential_reduce_fusion.9
  174.5 11.3 fusion.411
  214.2 66.2 %all-reduce.16.cloned.1.call-done = f32[1024,1024]{1,0:T(8,128)} async-done(((f32[1024,1024]{1,0:T(8,128)}), f32[1024,1024]{1,0:T(8,128)}) %all-reduce.16.cloned.1.call-update) | async-done | bytes 4194320 | tf_op jit(solution)/shard_map/psum | solution.py:302
  307.5 116.6 %all-reduce.34.cloned.1.call-done = (f32[512,1024]{1,0:T(8,128)}, f32[1024,1024]{1,0:T(8,128)}) async-done(((f32[512,1024]{1,0:T(8,128)}, f32[1024,1024]{1,0:T(8,128)}), (f32[512,1024]{1,0:T(8,128)}, f32[1024,1024]{1,0:T(8,128)})) %all-reduce.34.cloned.1.call-update) | async-done | bytes 6291472 | tf_op jit(solution)/shard_map/psum | solution.py:302
  440.8 40.3 %collective-permute-done.4 = bf16[1024,2,256]{2,0,1:T(8,128)(2,1)S(1)} collective-permute-done((bf16[1024,2,256]{2,0,1:T(8,128)(2,1)S(1)}, bf16[1024,2,256]{2,0,1:T(8,128)(2,1)S(1)}, u32[]{:S(2)}, u32[]{:S(2)}) %collective-permute-start.4) | collective-permute-done | bytes 1048608 | tf_op jit(solution)/shard_map/ppermute | solution.py:23
  486.1 12.6 fusion.63
  498.7 11.9 exponential_reduce_fusion.2
  513.6 12.8 fusion.254
  528.4 53.0 %all-reduce.18.cloned.1.call-done = f32[512,1024]{1,0:T(8,128)} async-done(((f32[512,1024]{1,0:T(8,128)}), f32[512,1024]{1,0:T(8,128)}) %all-reduce.18.cloned.1.call-update) | async-done | bytes 2097168 | tf_op jit(solution)/shard_map/psum | solution.py:302
  597.7 51.3 %all-reduce.20.cloned.1.call-done = f32[512,1024]{1,0:T(8,128)} async-done(((f32[512,1024]{1,0:T(8,128)}), f32[512,1024]{1,0:T(8,128)}) %all-reduce.20.cloned.1.call-update) | async-done | bytes 2097168 | tf_op jit(solution)/shard_map/psum | solution.py:302
  674.2 51.3 %all-reduce.22.cloned.1.call-done = f32[512,1024]{1,0:T(8,128)} async-done(((f32[512,1024]{1,0:T(8,128)}), f32[512,1024]{1,0:T(8,128)}) %all-reduce.22.cloned.1.call-update) | async-done | bytes 2097168 | tf_op jit(solution)/shard_map/psum | solution.py:306
  733.2 13.3 fusion.221
  746.5 17.5 %multiply_convert_fusion.1 = bf16[4,512,3072]{2,1,0:T(8,128)(2,1)} fusion(f32[4,512,3072]{2,1,0:T(8,128)} %get-tuple-element.576, f32[4,512]{1,0:T(4,128)S(1)} %bitcast.459, f32[4,512]{1,0:T(4,128)S(1)} %log_add_fusion.1, pred[512,3072]{1,0:T(8,128)(4,1)} %compare_and_fusion.2, bf16[512,4,64]{0,2,1:T(8,128)(2,1)S(1)} %bitcast.421, ...), kind=kOutput, calls=%fused_computation.84 | convolution fusion | flops 843055104 | bytes 41172992 | tf_op jit(solution)/shard_map/while/body/eval_jaxpr/qhd,khd->hqk/dot_general | solution.py:173
  777.0 87.7 %collective-permute-done.6 = f32[1024,2,256]{0,2,1:T(8,128)S(1)} collective-permute-done((f32[1024,2,256]{0,2,1:T(8,128)S(1)}, f32[1024,2,256]{0,2,1:T(8,128)S(1)}, u32[]{:S(2)}, u32[]{:S(2)}) %collective-permute-start.6) | collective-permute-done | bytes 2097184 | tf_op jit(solution)/shard_map/ppermute | solution.py:23
  880.5 75.5 %all-reduce.24.cloned.1.call-done = f32[1024,1024]{1,0:T(8,128)} async-done(((f32[1024,1024]{1,0:T(8,128)}), f32[1024,1024]{1,0:T(8,128)}) %all-reduce.24.cloned.1.call-update) | async-done | bytes 4194320 | tf_op jit(solution)/shard_map/psum | solution.py:429
  967.6 17.5 %fusion.100 = f32[1024,1024]{1,0:T(8,128)} fusion(bf16[1024,1024]{1,0:T(8,128)(2,1)} %param.37, f32[1024,1024]{1,0:T(8,128)} %copy-done.159, bf16[1024,1024]{1,0:T(8,128)(2,1)S(1)} %copy-done, f32[1024,1024]{1,0:T(8,128)} %copy-done.15, f32[1024]{0:T(1024)S(1)} %negate_multiply_fusion.5), kind=kOutput, calls=%fused_computation.215 | convolution fusion | flops 4372561920 | bytes 16781312 | tf_op jit(solution)/shard_map/qf,ef->qe/dot_general | solution.py:292
  992.4 118.6 %all-reduce.32.cloned.1.call-done = (f32[1024,1024]{1,0:T(8,128)}, f32[512,1024]{1,0:T(8,128)}) async-done(((f32[1024,1024]{1,0:T(8,128)}, f32[512,1024]{1,0:T(8,128)}), (f32[1024,1024]{1,0:T(8,128)}, f32[512,1024]{1,0:T(8,128)})) %all-reduce.32.cloned.1.call-update) | async-done | bytes 6291472 | tf_op jit(solution)/shard_map/psum | solution.py:306
  1151.6 138.8 %while.6 = (s32[]{:T(128)}, f32[3072,4,64]{0,2,1:T(8,128)}, f32[3072,4,64]{0,2,1:T(8,128)}, f32[30,4,64]{2,0,1:T(8,128)}, f32[30,4,64]{2,0,1:T(8,128)}, /*index=...) while((s32[]{:T(128)}, f32[3072,4,64]{0,2,1:T(8,128)}, ...), condition=%wide.region_43.44_spmd.clone, body=%wide.region_41.43_spmd.clone.sunk | while | flops 4137040384 | bytes 146749344 | solution.py:229
  1165.3 17.3 %multiply_convert_fusion.13 = bf16[4,512,3072]{2,1,0:T(8,128)(2,1)} fusion(f32[4,512,3072]{2,1,0:T(8,128)} %fusion.432, f32[4,512]{1,0:T(4,128)S(1)} %bitcast.433, f32[4,512]{1,0:T(4,128)S(1)} %dynamic-slice_bitcast_fusion.2, pred[512,3072]{1,0:T(8,128)(4,1)} %compare_and_fusion.7, bf16[3072,4,64]{0,2,1:T(8,128)(2,1)} %get-tuple-element.837, ...), kind=kOutput, calls=%fused_computation.26.clone.1 | convolution fusion | flops 843055104 | bytes 41172996 | tf_op jit(solution)/shard_map/while/body/eval_jaxpr/qhd,khd->hqk/dot_general | solution.py:173
  1205.2 14.0 fusion.435
  1233.5 17.3 %multiply_convert_fusion.13 = bf16[4,512,3072]{2,1,0:T(8,128)(2,1)} fusion(f32[4,512,3072]{2,1,0:T(8,128)} %fusion.432, f32[4,512]{1,0:T(4,128)S(1)} %bitcast.433, f32[4,512]{1,0:T(4,128)S(1)} %dynamic-slice_bitcast_fusion.2, pred[512,3072]{1,0:T(8,128)(4,1)} %compare_and_fusion.7, bf16[3072,4,64]{0,2,1:T(8,128)(2,1)} %get-tuple-element.837, ...), kind=kOutput, calls=%fused_computation.26.clone.1 | convolution fusion | flops 843055104 | bytes 41172996 | tf_op jit(solution)/shard_map/while/body/eval_jaxpr/qhd,khd->hqk/dot_general | solution.py:173
  1274.3 14.9 fusion.435
  1321.4 72.8 %collective-permute-done.10 = f32[512,2,256]{0,2,1:T(8,128)} collective-permute-done((f32[512,2,256]{0,2,1:T(8,128)}, f32[512,2,256]{0,2,1:T(8,128)}, u32[]{:S(2)}, u32[]{:S(2)}) %collective-permute-start.10) | collective-permute-done | bytes 1048608 | tf_op jit(solution)/shard_map/ppermute | solution.py:23
  1398.4 40.5 %collective-permute-done.8 = f32[1024,2,256]{0,2,1:T(8,128)} collective-permute-done((f32[1024,2,256]{0,2,1:T(8,128)}, f32[1024,2,256]{0,2,1:T(8,128)}, u32[]{:S(2)}, u32[]{:S(2)}) %collective-permute-start.8) | collective-permute-done | bytes 2097184 | tf_op jit(solution)/shard_map/ppermute | solution.py:23
  1459.3 107.6 %all-reduce.30.cloned.1.call-done = (f32[1024,1024]{1,0:T(8,128)}, f32[512,1024]{1,0:T(8,128)}) async-done(((f32[1024,1024]{1,0:T(8,128)}, f32[512,1024]{1,0:T(8,128)}), (f32[1024,1024]{1,0:T(8,128)}, f32[512,1024]{1,0:T(8,128)})) %all-reduce.30.cloned.1.call-update) | async-done | bytes 6291472 | tf_op jit(solution)/shard_map/psum | solution.py:306
  1575.1 100.7 %all-reduce.28.cloned.1.call-done = (f32[1024,128]{1,0:T(8,128)}, f32[128,1024]{1,0:T(8,128)}, f32[1024,128]{1,0:T(8,128)}, f32[128,1024]{1,0:T(8,128)}) async-done(((f32[1024,128]{1,0:T(8,128)}, f32[128,1024]{1,0:T(8,128)}, f32[1024,128]{1,0:T(8,128)}, f32[128,1024]{1,0:T(8,128)}), (f32[1024,128]{1,0:T(8,128)}, f32[128,1024]{1,0:T(8,128)}, f32[1024,128]{1,0:T(8,128)}, ...) | async-done | bytes 2097168 | tf_op jit(solution)/shard_map/psum | solution.py:461
  (626 shorter events, 422.3 us)
Async XLA Ops:
  7.2 283.5 %copy-start = (bf16[1024,1024]{1,0:T(8,128)(2,1)S(1)}, bf16[1024,1024]{1,0:T(8,128)(2,1)}, u32[]{:S(2)}) copy-start(bf16[1024,1024]{1,0:T(8,128)(2,1)} %param.38) | copy-start | bytes 6291460
  7.2 273.3 %all-reduce.16.cloned.1.call-start = ((), (), s32[]{:S(2)}) async-start(), calls=%async_computation | async-start | bytes 8388608 | tf_op jit(solution)/shard_map/psum | solution.py:302
  12.0 86.3 %collective-permute-start.2 = (bf16[1024,2,256]{2,0,1:T(8,128)(2,1)}, bf16[1024,2,256]{2,0,1:T(8,128)(2,1)}, u32[]{:S(2)}, u32[]{:S(2)}) collective-permute-start(bf16[1024,2,256]{2,0,1:T(8,128)(2,1)} %pad_maximum_fusion.6), channel_id=1, source_target_pairs={{0,4},{4,8},{8,12},{12,16},{16,20},{20,24},{24,28},{1,5},{5,9},{9,... | collective-permute-start | bytes 3145736 | tf_op jit(solution)/shard_map/ppermute | solution.py:23
  17.8 80.5 %collective-permute-start.3 = (bf16[1024,2,256]{2,0,1:T(8,128)(2,1)}, bf16[1024,2,256]{2,0,1:T(8,128)(2,1)}, u32[]{:S(2)}, u32[]{:S(2)}) collective-permute-start(bf16[1024,2,256]{2,0,1:T(8,128)(2,1)} %pad_maximum_fusion.6), channel_id=1, source_target_pairs={{4,0},{8,4},{12,8},{16,12},{20,16},{24,20},{28,24},{5,1},{9,5},{13... | collective-permute-start | bytes 3145736 | tf_op jit(solution)/shard_map/ppermute | solution.py:24
  20.9 63.6 %collective-permute-start = (bf16[512,2,256]{2,0,1:T(8,128)(2,1)}, bf16[512,2,256]{2,0,1:T(8,128)(2,1)}, u32[]{:S(2)}, u32[]{:S(2)}) collective-permute-start(bf16[512,2,256]{2,0,1:T(8,128)(2,1)} %pad_maximum_fusion.8), channel_id=1, source_target_pairs={{0,4},{4,8},{8,12},{12,16},{16,20},{20,24},{24,28},{1,5},{5,9},{9,... | collective-permute-start | bytes 1572872 | tf_op jit(solution)/shard_map/ppermute | solution.py:23
  26.3 58.2 %collective-permute-start.1 = (bf16[512,2,256]{2,0,1:T(8,128)(2,1)}, bf16[512,2,256]{2,0,1:T(8,128)(2,1)}, u32[]{:S(2)}, u32[]{:S(2)}) collective-permute-start(bf16[512,2,256]{2,0,1:T(8,128)(2,1)} %pad_maximum_fusion.8), channel_id=1, source_target_pairs={{4,0},{8,4},{12,8},{16,12},{20,16},{24,20},{28,24},{5,1},{9,5},{13... | collective-permute-start | bytes 1572872 | tf_op jit(solution)/shard_map/ppermute | solution.py:24
  187.1 118.1 %copy-start.48 = (s32[3072]{0:T(1024)}, s32[3072]{0:T(1024)S(1)}, u32[]{:S(2)}) copy-start(s32[3072]{0:T(1024)S(1)} %get-tuple-element.910) | copy-start | bytes 36868
  192.6 231.6 %all-reduce.34.cloned.1.call-start = ((), (), s32[]{:S(2)}) async-start(), calls=%async_computation.9 | async-start | bytes 12582912 | tf_op jit(solution)/shard_map/psum | solution.py:302
  283.8 140.4 %copy-start.111 = (f32[1024]{0:T(1024)}, f32[1024]{0:T(1024)S(1)}, u32[]{:S(2)}) copy-start(f32[1024]{0:T(1024)S(1)} %broadcast_multiply_fusion.1) | copy-start | bytes 12292
  284.4 139.8 %copy-start.129 = (f32[1024]{0:T(1024)}, f32[1024]{0:T(1024)S(1)}, u32[]{:S(2)}) copy-start(f32[1024]{0:T(1024)S(1)} %fusion.205) | copy-start | bytes 12292
  304.1 277.2 %all-reduce.18.cloned.1.call-start = ((), (), s32[]{:S(2)}) async-start(), calls=%async_computation.1 | async-start | bytes 4194304 | tf_op jit(solution)/shard_map/psum | solution.py:302
  305.2 276.1 %copy-start.121 = (f32[1,1024]{1,0:T(1,128)}, f32[1,1024]{1,0:T(1,128)S(1)}, u32[]{:S(2)}) copy-start(f32[1,1024]{1,0:T(1,128)S(1)} %get-tuple-element.560) | copy-start | bytes 12292
  432.9 48.2 %collective-permute-start.4 = (bf16[1024,2,256]{2,0,1:T(8,128)(2,1)S(1)}, bf16[1024,2,256]{2,0,1:T(8,128)(2,1)S(1)}, u32[]{:S(2)}, u32[]{:S(2)}) collective-permute-start(bf16[1024,2,256]{2,0,1:T(8,128)(2,1)S(1)} %pad_maximum_fusion.7), channel_id=1, source_target_pairs={{0,4},{4,8},{8,12},{12,16},{16,20},{20,24},{24,28},{1,5},{5,9},{9,... | collective-permute-start | bytes 3145736 | tf_op jit(solution)/shard_map/ppermute | solution.py:23
  436.5 44.6 %collective-permute-start.5 = (bf16[1024,2,256]{2,0,1:T(8,128)(2,1)S(1)}, bf16[1024,2,256]{2,0,1:T(8,128)(2,1)S(1)}, u32[]{:S(2)}, u32[]{:S(2)}) collective-permute-start(bf16[1024,2,256]{2,0,1:T(8,128)(2,1)S(1)} %pad_maximum_fusion.7), channel_id=1, source_target_pairs={{4,0},{8,4},{12,8},{16,12},{20,16},{24,20},{28,24},{5,1},{9,5},{13... | collective-permute-start | bytes 3145736 | tf_op jit(solution)/shard_map/ppermute | solution.py:24
  438.5 142.9 %copy-start.127 = (f32[512]{0:T(512)}, f32[512]{0:T(512)S(1)}, u32[]{:S(2)}) copy-start(f32[512]{0:T(512)S(1)} %broadcast_multiply_fusion.4) | copy-start | bytes 6148
  438.9 142.5 %copy-start.140 = (f32[512]{0:T(512)}, f32[512]{0:T(512)S(1)}, u32[]{:S(2)}) copy-start(f32[512]{0:T(512)S(1)} %fusion.207) | copy-start | bytes 6148
  528.2 120.9 %all-reduce.20.cloned.1.call-start = ((), (), s32[]{:S(2)}) async-start(), calls=%async_computation.2 | async-start | bytes 4194304 | tf_op jit(solution)/shard_map/psum | solution.py:302
  597.5 128.0 %all-reduce.22.cloned.1.call-start = ((), (), s32[]{:S(2)}) async-start(), calls=%async_computation.3 | async-start | bytes 4194304 | tf_op jit(solution)/shard_map/psum | solution.py:306
  673.9 282.1 %all-reduce.24.cloned.1.call-start = ((), (), s32[]{:S(2)}) async-start(), calls=%async_computation.4 | async-start | bytes 8388608 | tf_op jit(solution)/shard_map/psum | solution.py:429
  771.6 93.1 %collective-permute-start.6 = (f32[1024,2,256]{0,2,1:T(8,128)S(1)}, f32[1024,2,256]{0,2,1:T(8,128)S(1)}, u32[]{:S(2)}, u32[]{:S(2)}) collective-permute-start(f32[1024,2,256]{0,2,1:T(8,128)S(1)} %get-tuple-element.548), channel_id=1, source_target_pairs={{0,4},{4,8},{8,12},{12,16},{16,20},{20,24},{24,28},{1,5},{5,9},{9,... | collective-permute-start | bytes 6291464 | tf_op jit(solution)/shard_map/ppermute | solution.py:23
  775.1 89.6 %collective-permute-start.7 = (f32[1024,2,256]{0,2,1:T(8,128)S(1)}, f32[1024,2,256]{0,2,1:T(8,128)S(1)}, u32[]{:S(2)}, u32[]{:S(2)}) collective-permute-start(f32[1024,2,256]{0,2,1:T(8,128)S(1)} %get-tuple-element.549), channel_id=1, source_target_pairs={{4,0},{8,4},{12,8},{16,12},{20,16},{24,20},{28,24},{5,1},{9,5},{13... | collective-permute-start | bytes 6291464 | tf_op jit(solution)/shard_map/ppermute | solution.py:24
  869.1 241.8 %all-reduce.32.cloned.1.call-start = ((), (), s32[]{:S(2)}) async-start(), calls=%async_computation.8 | async-start | bytes 12582912 | tf_op jit(solution)/shard_map/psum | solution.py:306
  990.9 120.1 %copy-start.12 = (f32[512,1024]{1,0:T(8,128)S(1)}, f32[512,1024]{1,0:T(8,128)}, u32[]{:S(2)}) copy-start(f32[512,1024]{1,0:T(8,128)} %copy-done.11) | copy-start | bytes 6291460
  990.9 120.1 %copy-start.122 = (f32[1,1024]{1,0:T(1,128)S(1)}, f32[1,1024]{1,0:T(1,128)}, u32[]{:S(2)}) copy-start(f32[1,1024]{1,0:T(1,128)} %copy-done.121) | copy-start | bytes 12292
  990.9 120.1 %copy-start.128 = (f32[512]{0:T(512)S(1)}, f32[512]{0:T(512)}, u32[]{:S(2)}) copy-start(f32[512]{0:T(512)} %copy-done.127) | copy-start | bytes 6148
  990.9 463.9 %all-reduce.26.cloned.1.call-start = ((), (), s32[]{:S(2)}) async-start(), calls=%async_computation.5 | async-start | bytes 393216 | tf_op jit(solution)/shard_map/psum | solution.py:461
  1298.1 96.0 %collective-permute-start.10 = (f32[512,2,256]{0,2,1:T(8,128)}, f32[512,2,256]{0,2,1:T(8,128)}, u32[]{:S(2)}, u32[]{:S(2)}) collective-permute-start(f32[512,2,256]{0,2,1:T(8,128)} %get-tuple-element.550), channel_id=1, source_target_pairs={{0,4},{4,8},{8,12},{12,16},{16,20},{20,24},{24,28},{1,5},{5,9},{9,... | collective-permute-start | bytes 3145736 | tf_op jit(solution)/shard_map/ppermute | solution.py:23
  1302.6 91.5 %collective-permute-start.11 = (f32[512,2,256]{0,2,1:T(8,128)}, f32[512,2,256]{0,2,1:T(8,128)}, u32[]{:S(2)}, u32[]{:S(2)}) collective-permute-start(f32[512,2,256]{0,2,1:T(8,128)} %get-tuple-element.551), channel_id=1, source_target_pairs={{4,0},{8,4},{12,8},{16,12},{20,16},{24,20},{28,24},{5,1},{9,5},{13... | collective-permute-start | bytes 3145736 | tf_op jit(solution)/shard_map/ppermute | solution.py:24
  1306.3 132.6 %collective-permute-start.8 = (f32[1024,2,256]{0,2,1:T(8,128)}, f32[1024,2,256]{0,2,1:T(8,128)}, u32[]{:S(2)}, u32[]{:S(2)}) collective-permute-start(f32[1024,2,256]{0,2,1:T(8,128)} %get-tuple-element.546), channel_id=1, source_target_pairs={{0,4},{4,8},{8,12},{12,16},{16,20},{20,24},{24,28},{1,5},{5,9},{9,... | collective-permute-start | bytes 6291464 | tf_op jit(solution)/shard_map/ppermute | solution.py:23
  1312.1 126.8 %collective-permute-start.9 = (f32[1024,2,256]{0,2,1:T(8,128)}, f32[1024,2,256]{0,2,1:T(8,128)}, u32[]{:S(2)}, u32[]{:S(2)}) collective-permute-start(f32[1024,2,256]{0,2,1:T(8,128)} %get-tuple-element.547), channel_id=1, source_target_pairs={{4,0},{8,4},{12,8},{16,12},{20,16},{24,20},{28,24},{5,1},{9,5},{13... | collective-permute-start | bytes 6291464 | tf_op jit(solution)/shard_map/ppermute | solution.py:24
  1314.1 252.8 %all-reduce.30.cloned.1.call-start = ((), (), s32[]{:S(2)}) async-start(), calls=%async_computation.7 | async-start | bytes 12582912 | tf_op jit(solution)/shard_map/psum | solution.py:306
  1445.4 230.4 %all-reduce.28.cloned.1.call-start = ((), (), s32[]{:S(2)}) async-start(), calls=%async_computation.6 | async-start | bytes 4194304 | tf_op jit(solution)/shard_map/psum | solution.py:461
  (163 other events, 1978.2 us)
Sparse Core Ops, SparseCore 0:
  192.7 87.6 all-reduce.15
  304.3 119.8 all-reduce.33
  528.3 53.0 all-reduce.17
  597.6 51.4 all-reduce.19
  674.0 51.4 all-reduce.21
  869.2 86.7 all-reduce.23
  991.1 119.8 all-reduce.31
  1314.2 122.9 all-reduce.25
  1445.5 121.3 all-reduce.29
  1571.9 103.8 all-reduce.27
where the time goes:
time: 1700 us; the launch traced here: 1690 us
  waiting for transfers between devices  1030 us (61%)
  matrix products  399 us (23%)
  other arithmetic  127 us (7%)
  local copies, waits for them, and re-layouts  78.3 us (5%)
  starting transfers between devices  38.4 us (2%)
    ppermute x6, waiting for transfers between devices, extended(): before = lax.ppermute(last, axis, up)  288 us
    psum x4, waiting for transfers between devices, branch_total(): return lax.psum(piece_sum, 'tp')  287 us
    psum x3, waiting for transfers between devices, input_total(): return lax.psum(piece_sum, 'tp')  277 us
    psum x2, waiting for transfers between devices, on_device(): lax.psum((encoder_prefix_gradient, encoder_down_gradient, encoder_up_grad...  101 us
    psum x1, waiting for transfers between devices, on_device(): query_total, encoded_gradient = lax.psum((query_piece, key_piece), 'tp')  75.5 us
    dot_general x6, matrix products, window_scores(): jnp.einsum('qhd,khd->hqk', queries, key_heads, preferred_element_type=jnp...  65.7 us
    dot_general x4, matrix products, backward_block(): jnp.einsum('qhd,khd->hqk', block_grad, value_heads, preferred_element_typ...  58.4 us
    dot_general x4, matrix products, backward_block(): jnp.einsum('hqk,qhd->khd', main_chances.astype(jnp.bfloat16), block_grad,...  50.7 us
  transfers between devices with their start and end apart: 22, of which 14 were waited for; matrix products, arithmetic and copies ran while one was open for 6% of the time, Pallas kernels for 0%

commit v1 on v0

v1 whole, which is shorter than its diff:
```python
from functools import partial

import jax
import jax.numpy as jnp
from jax import lax
from jax.experimental import pallas as pl
from jax.experimental.pallas import tpu as pltpu
from jax.sharding import PartitionSpec as P

HEAD_DIM = 64
EPSILON = 1e-05
NEGATIVE = -1e30
HEADS = 4
KEY_BLOCK = 256
PREFIX = 30
PREFIX_ROWS = 32
SEGMENT = 64
MESH = pl.DeviceIdType.MESH
F32 = jnp.float32
BF16 = jnp.bfloat16
VMEM_BYTES = 56 * 2**20


def mm(left, right):
    return jnp.dot(left, right, preferred_element_type=F32)


def mm_nt(left, right):
    return lax.dot_general(left, right, (((1,), (1,)), ((), ())), preferred_element_type=F32)


def mm_tn(left, right):
    return lax.dot_general(left, right, (((0,), (0,)), ((), ())), preferred_element_type=F32)


def normalize(inputs, scaling):
    centered = inputs - jnp.mean(inputs, axis=-1, keepdims=True)
    spread = lax.rsqrt(jnp.mean(centered * centered, axis=-1, keepdims=True) + EPSILON)
    return scaling * (centered * spread)


def normalize_back(inputs, scaling, gradient):
    centered = inputs - jnp.mean(inputs, axis=-1, keepdims=True)
    spread = lax.rsqrt(jnp.mean(centered * centered, axis=-1, keepdims=True) + EPSILON)
    unit = centered * spread
    scaled = gradient * scaling
    first = jnp.mean(scaled, axis=-1, keepdims=True)
    second = jnp.mean(scaled * unit, axis=-1, keepdims=True)
    return spread * (scaled - first - unit * second)


def gelu_parts(inputs):
    chance = 0.5 * (1.0 + lax.erf(inputs * (0.5**0.5)))
    density = jnp.exp(-0.5 * inputs * inputs) * 0.3989422804014327
    return (inputs * chance).astype(BF16), (chance + inputs * density).astype(BF16)


def project_kernel(x_ref, w_ref, q_ref, kv_ref):
    rows = x_ref[...]
    q_ref[...] = mm(rows, w_ref[0]).astype(BF16)
    kv_ref[0] = mm(rows, w_ref[1]).astype(BF16)
    kv_ref[1] = mm(rows, w_ref[2]).astype(BF16)


def project(inputs, weights):
    rows, width = inputs.shape
    block = 256
    cols = weights.shape[2]
    return pl.pallas_call(
        project_kernel,
        grid=(rows // block,),
        in_specs=[
            pl.BlockSpec((block, width), lambda i: (i, 0)),
            pl.BlockSpec(weights.shape, lambda i: (0, 0, 0)),
        ],
        out_specs=[
            pl.BlockSpec((block, cols), lambda i: (i, 0)),
            pl.BlockSpec((2, block, cols), lambda i: (0, i, 0)),
        ],
        out_shape=[
            jax.ShapeDtypeStruct((rows, cols), BF16),
            jax.ShapeDtypeStruct((2, rows, cols), BF16),
        ],
        compiler_params=pltpu.CompilerParams(vmem_limit_bytes=VMEM_BYTES),
        cost_estimate=pl.CostEstimate(
            flops=6 * rows * width * cols, bytes_accessed=8 * rows * cols + 6 * width * cols, transcendentals=0
        ),
    )(inputs, weights)


def by_heads(rows, lane_head):
    zero = jnp.zeros_like(rows)
    return jnp.concatenate([jnp.where(lane_head == h, rows, zero) for h in range(HEADS)], axis=0)


def head_bias(kd_ref, qd_ref, start, first_query, halo, block, causal):
    key_doc = kd_ref[pl.ds(start, KEY_BLOCK), :]
    allowed = key_doc == qd_ref[0]
    if causal:
        key_place = start - halo + lax.broadcasted_iota(jnp.int32, (KEY_BLOCK, block), 0)
        query_place = first_query + lax.broadcasted_iota(jnp.int32, (KEY_BLOCK, block), 1)
        allowed = allowed & (key_place <= query_place)
    bias = jnp.where(allowed, 0.0, NEGATIVE)
    return jnp.concatenate([bias] * HEADS, axis=1)


def prefix_scores(pre_ref, stacked):
    scores = mm_nt(pre_ref[0], stacked)
    row = lax.broadcasted_iota(jnp.int32, scores.shape, 0)
    return jnp.where(row < PREFIX, scores, NEGATIVE)


def fill_window(window, parts, index):
    at = 0
    for part in parts:
        size = part.shape[1]
        window[at : at + size, :] = part[index]
        at += size


def attend_kernel(
    halo, causal, lo_ref, hi_ref, q_ref, bef_ref, own_ref, aft_ref, pre_ref, qd_ref, kd_ref,
    wide_ref, low_ref, total_ref, keys, values, blended,
):
    i = pl.program_id(0)
    block = q_ref.shape[0]
    parts = (bef_ref, own_ref, aft_ref)

    @pl.when(i == 0)
    def _():
        fill_window(keys, parts, 0)
        at = 0
        for part in parts:
            for k in range(part.shape[1] // KEY_BLOCK):
                values[at] = part[1, k * KEY_BLOCK : (k + 1) * KEY_BLOCK, :].T
                at += 1

    lane_head = lax.broadcasted_iota(jnp.int32, q_ref.shape, 1) // HEAD_DIM
    stacked = by_heads(q_ref[...] * jnp.asarray(HEAD_DIM**-0.5, BF16), lane_head)
    scores = prefix_scores(pre_ref, stacked)
    highest = jnp.max(scores, axis=0, keepdims=True)
    chances = jnp.exp(scores - highest)
    summed = jnp.sum(chances, axis=0, keepdims=True)
    low = chances.astype(BF16)
    pre_values = pre_ref[1].T
    for h in range(HEADS):
        rows = slice(h * HEAD_DIM, (h + 1) * HEAD_DIM)
        blended[rows, :] = mm(pre_values[rows, :], low[:, h * block : (h + 1) * block])

    def step(kb, carry):
        highest, summed = carry
        start = pl.multiple_of(kb * KEY_BLOCK, KEY_BLOCK)
        scores = mm_nt(keys[pl.ds(start, KEY_BLOCK), :], stacked)
        scores = scores + head_bias(kd_ref, qd_ref, start, i * block, halo, block, causal)
        top = jnp.maximum(highest, jnp.max(scores, axis=0, keepdims=True))
        fade = jnp.exp(highest - top)
        chances = jnp.exp(scores - top)
        summed = summed * fade + jnp.sum(chances, axis=0, keepdims=True)
        low = chances.astype(BF16)
        for h in range(HEADS):
            rows = slice(h * HEAD_DIM, (h + 1) * HEAD_DIM)
            cols = slice(h * block, (h + 1) * block)
            blended[rows, :] = blended[rows, :] * fade[:, cols] + mm(values[kb, rows, :], low[:, cols])
        return top, summed

    highest, summed = lax.fori_loop(lo_ref[i], hi_ref[i], step, (highest, summed))
    total_ref[0] = highest + jnp.log(summed)
    inverse = 1.0 / summed
    for h in range(HEADS):
        rows = slice(h * HEAD_DIM, (h + 1) * HEAD_DIM)
        blended[rows, :] = blended[rows, :] * inverse[:, h * block : (h + 1) * block]
    result = blended[...].T
    wide_ref[...] = result
    low_ref[...] = result.astype(BF16)


def attend(queries, parts, prefix, docs, causal):
    query_doc, key_doc, lo, hi = docs
    rows, cols = queries.shape
    count, _, block = query_doc.shape
    window = key_doc.shape[0]
    halo = parts[0].shape[1]

    def whole(array):
        return pl.BlockSpec(array.shape, lambda i, *_: (0,) * array.ndim)

    return pl.pallas_call(
        partial(attend_kernel, halo, causal),
        grid_spec=pltpu.PrefetchScalarGridSpec(
            num_scalar_prefetch=2,
            grid=(count,),
            in_specs=[
                pl.BlockSpec((block, cols), lambda i, *_: (i, 0)),
                whole(parts[0]),
                whole(parts[1]),
                whole(parts[2]),
                whole(prefix),
                pl.BlockSpec((1, 1, block), lambda i, *_: (i, 0, 0)),
                whole(key_doc),
            ],
            out_specs=[
                pl.BlockSpec((block, cols), lambda i, *_: (i, 0)),
                pl.BlockSpec((block, cols), lambda i, *_: (i, 0)),
                pl.BlockSpec((1, 1, HEADS * block), lambda i, *_: (i, 0, 0)),
            ],
            scratch_shapes=[
                pltpu.VMEM((window, cols), BF16),
                pltpu.VMEM((window // KEY_BLOCK, cols, KEY_BLOCK), BF16),
                pltpu.VMEM((cols, block), F32),
            ],
        ),
        out_shape=[
            jax.ShapeDtypeStruct((rows, cols), F32),
            jax.ShapeDtypeStruct((rows, cols), BF16),
            jax.ShapeDtypeStruct((count, 1, HEADS * block), F32),
        ],
        compiler_params=pltpu.CompilerParams(vmem_limit_bytes=VMEM_BYTES),
        cost_estimate=pl.CostEstimate(
            flops=16 * rows * 1024 * cols, bytes_accessed=8 * window * cols, transcendentals=4 * rows * 1024
        ),
    )(lo, hi, queries, *parts, prefix, query_doc, key_doc)


def attend_back_kernel(
    halo, causal, lo_ref, hi_ref, q_ref, g_ref, wide_ref, total_ref, bef_ref, own_ref, aft_ref, pre_ref,
    qd_ref, kd_ref, dq_ref, dbef_ref, down_ref, daft_ref, dpre_ref,
    keys, values, turned, key_sum, value_sum, query_sum, prefix_sum,
):
    i = pl.program_id(0)
    block = q_ref.shape[0]
    parts = (bef_ref, own_ref, aft_ref)

    @pl.when(i == 0)
    def _():
        fill_window(keys, parts, 0)
        fill_window(values, parts, 1)
        at = 0
        for part in parts:
            for k in range(part.shape[1] // KEY_BLOCK):
                turned[at] = part[0, k * KEY_BLOCK : (k + 1) * KEY_BLOCK, :].T
                at += 1
        key_sum[...] = jnp.zeros_like(key_sum)
        value_sum[...] = jnp.zeros_like(value_sum)
        prefix_sum[...] = jnp.zeros_like(prefix_sum)

    lane_head = lax.broadcasted_iota(jnp.int32, q_ref.shape, 1) // HEAD_DIM
    stacked = by_heads(q_ref[...] * jnp.asarray(HEAD_DIM**-0.5, BF16), lane_head)
    grads = by_heads(g_ref[...], lane_head)
    mixed = (g_ref[...].astype(F32) * wide_ref[...]).T
    offsets = jnp.concatenate(
        [
            jnp.sum(mixed[h * HEAD_DIM : (h + 1) * HEAD_DIM, :], axis=0, keepdims=True)
            for h in range(HEADS)
        ],
        axis=1,
    )
    total = total_ref[0]
    chances = jnp.exp(prefix_scores(pre_ref, stacked) - total)
    score_grad = (chances * (mm_nt(pre_ref[1], grads) - offsets)).astype(BF16)
    prefix_sum[0] += mm(score_grad, stacked)
    prefix_sum[1] += mm(chances.astype(BF16), grads)
    pre_keys = pre_ref[0].T
    for h in range(HEADS):
        rows = slice(h * HEAD_DIM, (h + 1) * HEAD_DIM)
        query_sum[rows, :] = mm(pre_keys[rows, :], score_grad[:, h * block : (h + 1) * block])

    def step(kb, carry):
        start = pl.multiple_of(kb * KEY_BLOCK, KEY_BLOCK)
        here = pl.ds(start, KEY_BLOCK)
        scores = mm_nt(keys[here, :], stacked)
        scores = scores + head_bias(kd_ref, qd_ref, start, i * block, halo, block, causal)
        chances = jnp.exp(scores - total)
        score_grad = (chances * (mm_nt(values[here, :], grads) - offsets)).astype(BF16)
        key_sum[here, :] += mm(score_grad, stacked)
        value_sum[here, :] += mm(chances.astype(BF16), grads)
        for h in range(HEADS):
            rows = slice(h * HEAD_DIM, (h + 1) * HEAD_DIM)
            query_sum[rows, :] += mm(turned[kb, rows, :], score_grad[:, h * block : (h + 1) * block])
        return carry

    lax.fori_loop(lo_ref[i], hi_ref[i], step, 0)
    dq_ref[...] = (query_sum[...].T * HEAD_DIM**-0.5).astype(BF16)

    @pl.when(i == pl.num_programs(0) - 1)
    def _():
        at = 0
        for part in (dbef_ref, down_ref, daft_ref):
            size = part.shape[1]
            part[0] = key_sum[at : at + size, :].astype(part.dtype)
            part[1] = value_sum[at : at + size, :].astype(part.dtype)
            at += size
        dpre_ref[...] = prefix_sum[...]


def attend_back(queries, grads, wide, total, parts, prefix, docs, causal):
    query_doc, key_doc, lo, hi = docs
    rows, cols = queries.shape
    count, _, block = query_doc.shape
    window = key_doc.shape[0]
    halo = parts[0].shape[1]

    def whole(shape):
        return pl.BlockSpec(shape, lambda i, *_: (0,) * len(shape))

    def blocked():
        return pl.BlockSpec((block, cols), lambda i, *_: (i, 0))

    return pl.pallas_call(
        partial(attend_back_kernel, halo, causal),
        grid_spec=pltpu.PrefetchScalarGridSpec(
            num_scalar_prefetch=2,
            grid=(count,),
            in_specs=[
                blocked(),
                blocked(),
                blocked(),
                pl.BlockSpec((1, 1, HEADS * block), lambda i, *_: (i, 0, 0)),
                whole(parts[0].shape),
                whole(parts[1].shape),
                whole(parts[2].shape),
                whole(prefix.shape),
                pl.BlockSpec((1, 1, block), lambda i, *_: (i, 0, 0)),
                whole(key_doc.shape),
            ],
            out_specs=[
                blocked(),
                whole(parts[0].shape),
                whole(parts[1].shape),
                whole(parts[2].shape),
                whole(prefix.shape),
            ],
            scratch_shapes=[
                pltpu.VMEM((window, cols), BF16),
                pltpu.VMEM((window, cols), BF16),
                pltpu.VMEM((window // KEY_BLOCK, cols, KEY_BLOCK), BF16),
                pltpu.VMEM((window, cols), F32),
                pltpu.VMEM((window, cols), F32),
                pltpu.VMEM((cols, block), F32),
                pltpu.VMEM(prefix.shape, F32),
            ],
        ),
        out_shape=[
            jax.ShapeDtypeStruct((rows, cols), BF16),
            jax.ShapeDtypeStruct(parts[0].shape, BF16),
            jax.ShapeDtypeStruct(parts[1].shape, F32),
            jax.ShapeDtypeStruct(parts[2].shape, BF16),
            jax.ShapeDtypeStruct(prefix.shape, F32),
        ],
        compiler_params=pltpu.CompilerParams(vmem_limit_bytes=VMEM_BYTES),
        cost_estimate=pl.CostEstimate(
            flops=40 * rows * 1024 * cols, bytes_accessed=16 * window * cols, transcendentals=4 * rows * 1024
        ),
    )(lo, hi, queries, grads, wide, total, *parts, prefix, query_doc, key_doc)


class Place:
    def __init__(self, n_seq):
        self.s = lax.axis_index("seq")
        self.t = lax.axis_index("tp")
        self.core = self.t % 2
        self.other = 1 - self.core
        self.twin_t = self.t + 1 - 2 * self.core
        self.across_t = (self.t + 2) % 4
        self.corner_t = 3 - self.t
        self.twin = (self.s, self.twin_t)
        self.across = (self.s, self.across_t)
        self.corner = (self.s, self.corner_t)
        self.after = ((self.s + 1) % n_seq, self.t)
        self.before = ((self.s + n_seq - 1) % n_seq, self.t)

    def greet(self, partners):
        barrier = pltpu.get_barrier_semaphore()
        for partner in partners:
            pl.semaphore_signal(barrier, inc=1, device_id=partner, device_id_type=MESH)
        pl.semaphore_wait(barrier, len(partners))


class Sems:
    def __init__(self, send, receive):
        self.send, self.receive, self.used = send, receive, 0

    def take(self):
        kind = self.used
        self.used += 1
        return kind


def remote(sems, kind, j, src, dst, device):
    return pltpu.make_async_remote_copy(
        src_ref=src,
        dst_ref=dst,
        send_sem=sems.send.at[kind, j],
        recv_sem=sems.receive.at[kind, j],
        device_id=device,
        device_id_type=MESH,
    )


def span(j):
    return pl.ds(pl.multiple_of(j * SEGMENT, SEGMENT), SEGMENT)


class Twins:
    def __init__(self, place, sems, buf):
        self.place, self.sems, self.buf, self.kind = place, sems, buf, sems.take()

    def copy(self, j, half):
        part = self.buf.at[half, span(j)]
        return remote(self.sems, self.kind, j, part, part, self.place.twin)

    def put(self, j, value):
        self.buf[self.place.core, span(j)] = value
        self.copy(j, self.place.core).start()

    def wait(self, j):
        self.copy(j, self.place.other).wait_recv()

    def both(self, j):
        return jnp.concatenate([self.buf[self.place.core, span(j)], self.buf[self.place.other, span(j)]], axis=0)

    def drain(self, j):
        self.copy(j, self.place.core).wait_send()


class Total:
    SHAPES = staticmethod(
        lambda half: [
            pltpu.VMEM((half, 1024), F32),
            pltpu.VMEM((half, 1024), BF16),
            pltpu.VMEM((half, 1024), BF16),
            pltpu.VMEM((half, 1024), BF16),
            pltpu.VMEM((half, 1024), BF16),
        ]
    )

    def __init__(self, place, sems, refs):
        self.place, self.sems = place, sems
        self.mine, self.away, self.came, self.chip, self.far = refs
        self.kind_twin, self.kind_across = sems.take(), sems.take()

    def twin_copy(self, j):
        rows = span(j)
        return remote(self.sems, self.kind_twin, j, self.away.at[rows], self.came.at[rows], self.place.twin)

    def across_copy(self, j):
        rows = span(j)
        return remote(self.sems, self.kind_across, j, self.chip.at[rows], self.far.at[rows], self.place.across)

    def put(self, j, value):
        self.mine[span(j)] = value[:SEGMENT]
        self.away[span(j)] = value[SEGMENT:].astype(BF16)
        self.twin_copy(j).start()

    def middle(self, j):
        self.twin_copy(j).wait_recv()
        self.chip[span(j)] = (self.mine[span(j)] + self.came[span(j)].astype(F32)).astype(BF16)
        self.across_copy(j).start()

    def get(self, j):
        self.across_copy(j).wait_recv()
        return self.chip[span(j)].astype(F32) + self.far[span(j)].astype(F32)

    def drain(self, j):
        self.twin_copy(j).wait_send()
        self.across_copy(j).wait_send()


class Heads:
    def __init__(self, place, sems, own, buf):
        self.place, self.sems, self.own, self.buf = place, sems, own, buf
        self.kinds = [sems.take() for _ in range(3)]

    def copies(self, j):
        p, rows = self.place, span(j)
        landing = self.buf.at[p.t, rows]
        return [
            remote(self.sems, self.kinds[0], j, self.own.at[p.core, rows], landing, p.across),
            remote(self.sems, self.kinds[1], j, self.own.at[p.other, rows], landing, p.corner),
            remote(self.sems, self.kinds[2], j, self.own.at[p.other, rows], landing, p.twin),
        ]

    def send(self, j):
        for copy in self.copies(j):
            copy.start()
        self.buf[self.place.t, span(j)] = self.own[self.place.core, span(j)]

    def wait(self, j):
        p, rows = self.place, span(j)
        for kind, source, device in zip(
            self.kinds, (p.across_t, p.corner_t, p.twin_t), (p.across, p.corner, p.twin)
        ):
            part = self.buf.at[source, rows]
            remote(self.sems, kind, j, part, part, device).wait_recv()

    def mix(self, j, weight):
        rows = span(j)
        total = mm(self.buf[0, rows], weight[0])
        for k in range(1, 4):
            total = total + mm(self.buf[k, rows], weight[k])
        return total

    def drain(self, j):
        for copy in self.copies(j):
            copy.wait_send()


class Halo:
    def __init__(self, place, sems, rows, halo):
        self.place, self.sems, self.rows, self.halo = place, sems, rows, halo
        self.half = rows // 2
        self.up = [sems.take() if hh * self.half >= rows - halo else None for hh in range(2)]
        self.down = [sems.take() if hh * self.half < halo else None for hh in range(2)]

    def place_up(self, hh, j):
        return span(j + (hh * self.half - (self.rows - self.halo)) // SEGMENT)

    def place_down(self, hh, j):
        return span(j + hh * self.half // SEGMENT)

    def out_copies(self, j, own, before, after):
        copies = []
        for hh in range(2):
            src = own.at[:, self.place_down(hh, j)]
            if self.up[hh] is not None:
                dst = before.at[:, self.place_up(hh, j)]
                copies.append(remote(self.sems, self.up[hh], j, src, dst, self.place.after))
            if self.down[hh] is not None:
                dst = after.at[:, self.place_down(hh, j)]
                copies.append(remote(self.sems, self.down[hh], j, src, dst, self.place.before))
        return copies

    def back_copies(self, j, before, after, from_before, from_after):
        copies = []
        for hh in range(2):
            if self.up[hh] is not None:
                where = self.place_up(hh, j)
                copies.append(
                    remote(self.sems, self.up[hh], j, before.at[:, where], from_after.at[:, where], self.place.before)
                )
            if self.down[hh] is not None:
                where = self.place_down(hh, j)
                copies.append(
                    remote(self.sems, self.down[hh], j, after.at[:, where], from_before.at[:, where], self.place.after)
                )
        return copies

    def gathered(self, j, hh, own, from_before, from_after):
        total = own[:, self.place_down(hh, j)]
        if self.down[hh] is not None:
            total = total + from_before[:, self.place_down(hh, j)].astype(F32)
        if self.up[hh] is not None:
            total = total + from_after[:, self.place_up(hh, j)].astype(F32)
        return total


def pipeline(n, stages):
    last = max(delay for delay, _ in stages)

    def step(s, carry):
        for delay, stage in stages:
            pl.when((s >= delay) & (s < n + delay))(partial(stage, s - delay))
        return carry

    lax.fori_loop(0, n + last, step, 0)


def each(n, *actions):
    def step(j, carry):
        for action in actions:
            action(j)
        return carry

    lax.fori_loop(0, n, step, 0)


def exchange_call(kernel, cid, outs, scratch, kinds, n, flops, args):
    vmem = pl.BlockSpec(memory_space=pltpu.VMEM)
    moved = sum(a.size * a.dtype.itemsize for a in args)
    return pl.pallas_call(
        kernel,
        in_specs=[vmem] * len(args),
        out_specs=[vmem] * len(outs),
        out_shape=[jax.ShapeDtypeStruct(shape, kind) for shape, kind in outs],
        scratch_shapes=scratch + [pltpu.SemaphoreType.DMA((kinds, n)), pltpu.SemaphoreType.DMA((kinds, n))],
        compiler_params=pltpu.CompilerParams(
            collective_id=cid, has_side_effects=True, vmem_limit_bytes=VMEM_BYTES
        ),
        cost_estimate=pl.CostEstimate(flops=flops, bytes_accessed=moved, transcendentals=0),
    )(*args)


def feed_rows(rows, w1, w2, wd, wu):
    inner, inner_slope = gelu_parts(mm(rows, w1[...]))
    side, side_slope = gelu_parts(mm(rows, wd[...]))
    return mm(inner, w2[...]) + 4.0 * mm(side, wu[...]), inner_slope, side, side_slope


def feed_rows_back(grads, rows, inner_slope, side, side_slope, w1, w2, wd, wu):
    four = (4.0 * grads.astype(F32)).astype(BF16)
    grad_inner = (inner_slope.astype(F32) * mm_nt(grads, w2[...])).astype(BF16)
    grad_side = (side_slope.astype(F32) * mm_nt(four, wu[...])).astype(BF16)
    piece = mm_nt(grad_inner, w1[...]) + mm_nt(grad_side, wd[...])
    return piece, mm_tn(rows, grad_side), mm_tn(side, four)


def encoder_forward_kernel(
    n_seq, halo_rows, a, x, gains, wo, w1, w2, wd, wu, wkv,
    e1, e3, hidden, inner_slope, side, side_slope, kv, before, after,
    heads_buf, e2, s0, s1, s2, s3, s4, encoded, send, receive,
):
    place, sems = Place(n_seq), Sems(send, receive)
    half = e1.shape[0]
    n = half // SEGMENT
    heads = Heads(place, sems, a, heads_buf)
    low = Twins(place, sems, hidden)
    total = Total(place, sems, (s0, s1, s2, s3, s4))
    low_encoded = Twins(place, sems, encoded)
    halo = Halo(place, sems, 2 * half, halo_rows)
    place.greet([place.twin, place.across, place.corner, place.before, place.after])
    each(n, heads.send)

    def mix(j):
        heads.wait(j)
        rows = span(j)
        first = x[place.core, rows].astype(F32) + heads.mix(j, wo)
        e1[rows] = first
        middle = normalize(first, gains[0:1])
        e2[rows] = middle
        low.put(j, middle.astype(BF16))

    def feed(j):
        low.wait(j)
        piece, slope, side_rows, slope_side = feed_rows(low.both(j), w1, w2, wd, wu)
        inner_slope[j] = slope
        side[j] = side_rows
        side_slope[j] = slope_side
        total.put(j, piece)

    def finish(j):
        rows = span(j)
        second = e2[rows] + total.get(j)
        e3[rows] = second
        low_encoded.put(j, normalize(second, gains[1:2]).astype(BF16))

    def memory(j):
        low_encoded.wait(j)
        rows = low_encoded.both(j)
        for i in range(2):
            made = mm(rows, wkv[i]).astype(BF16)
            kv[i, span(j + place.core * n)] = made[:SEGMENT]
            kv[i, span(j + place.other * n)] = made[SEGMENT:]
        for copy in halo.out_copies(j, kv, before, after):
            copy.start()

    pipeline(n, [(2, total.middle), (0, mix), (1, feed), (4, finish), (5, memory)])

    def arrived(j):
        for copy in halo.out_copies(j, kv, before, after):
            copy.wait()

    each(n, heads.drain, low.drain, total.drain, low_encoded.drain, arrived)


def decoder_self_kernel(n_seq, a, x, gains, wo, wq, t1, t2, q, heads_buf, hidden, send, receive):
    place, sems = Place(n_seq), Sems(send, receive)
    half = t1.shape[0]
    n = half // SEGMENT
    heads = Heads(place, sems, a, heads_buf)
    low = Twins(place, sems, hidden)
    place.greet([place.twin, place.across, place.corner])
    each(n, heads.send)

    def mix(j):
        heads.wait(j)
        rows = span(j)
        first = x[place.core, rows].astype(F32) + heads.mix(j, wo)
        t1[rows] = first
        middle = normalize(first, gains[0:1])
        t2[rows] = middle
        low.put(j, middle.astype(BF16))

    def query(j):
        low.wait(j)
        made = mm(low.both(j), wq[...]).astype(BF16)
        q[place.core, span(j)] = made[:SEGMENT]
        q[place.other, span(j)] = made[SEGMENT:]

    pipeline(n, [(0, mix), (1, query)])
    each(n, heads.drain, low.drain)


def decoder_chain_kernel(
    n_seq, a, t2, real, cotangent, gains, wo, w1, w2, wd, wu, mixing,
    decoded, g2, da, down_grad, up_grad,
    heads_buf, t3, t4, g3, hidden, low_g3, low_g2, inner_slope, side, side_slope,
    f0, f1, f2, f3, f4, b0, b1, b2, b3, b4, send, receive,
):
    place, sems = Place(n_seq), Sems(send, receive)
    half = t2.shape[0]
    n = half // SEGMENT
    heads = Heads(place, sems, a, heads_buf)
    low = Twins(place, sems, hidden)
    ahead = Total(place, sems, (f0, f1, f2, f3, f4))
    result = Twins(place, sems, decoded)
    back3 = Twins(place, sems, low_g3)
    behind = Total(place, sems, (b0, b1, b2, b3, b4))
    back2 = Twins(place, sems, low_g2)
    place.greet([place.twin, place.across, place.corner])
    each(n, heads.send)
    down_grad[...] = jnp.zeros_like(down_grad)
    up_grad[...] = jnp.zeros_like(up_grad)

    def mix(j):
        heads.wait(j)
        rows = span(j)
        second = t2[rows] + heads.mix(j, wo)
        t3[rows] = second
        late = normalize(second, gains[1:2])
        t4[rows] = late
        low.put(j, late.astype(BF16))

    def feed(j):
        low.wait(j)
        piece, slope, side_rows, slope_side = feed_rows(low.both(j), w1, w2, wd, wu)
        inner_slope[j] = slope
        side[j] = side_rows
        side_slope[j] = slope_side
        ahead.put(j, piece)

    def turn(j):
        rows = span(j)
        third = t4[rows] + ahead.get(j)
        mask = real[place.core, rows]
        result.put(j, normalize(third, gains[2:3]) * mask)
        grad = normalize_back(third, gains[2:3], cotangent[place.core, rows].astype(F32) * mask)
        g3[rows] = grad
        back3.put(j, grad.astype(BF16))

    def feed_back(j):
        back3.wait(j)
        piece, down, up = feed_rows_back(
            back3.both(j), low.both(j), inner_slope[j], side[j], side_slope[j], w1, w2, wd, wu
        )
        down_grad[...] += down
        up_grad[...] += up
        behind.put(j, piece)

    def finish(j):
        rows = span(j)
        grad = normalize_back(t3[rows], gains[1:2], g3[rows] + behind.get(j))
        g2[rows] = grad
        back2.put(j, grad.astype(BF16))

    def heads_back(j):
        back2.wait(j)
        made = mm_nt(back2.both(j), mixing[...]).astype(BF16)
        da[place.core, span(j)] = made[:SEGMENT]
        da[place.other, span(j)] = made[SEGMENT:]

    pipeline(
        n,
        [
            (2, ahead.middle),
            (6, behind.middle),
            (0, mix),
            (1, feed),
            (4, turn),
            (5, feed_back),
            (8, finish),
            (9, heads_back),
        ],
    )
    each(
        n, heads.drain, low.drain, ahead.drain, result.drain, result.wait, back3.drain, behind.drain, back2.drain
    )


def decoder_query_back_kernel(
    n_seq, dq, g2, t1, gains, wq, mixing, g1, da, low_g1, s0, s1, s2, s3, s4, send, receive
):
    place, sems = Place(n_seq), Sems(send, receive)
    half = t1.shape[0]
    n = half // SEGMENT
    total = Total(place, sems, (s0, s1, s2, s3, s4))
    back = Twins(place, sems, low_g1)
    place.greet([place.twin, place.across])

    def start(j):
        rows = jnp.concatenate([dq[place.core, span(j)], dq[place.other, span(j)]], axis=0)
        total.put(j, mm_nt(rows, wq[...]))

    def finish(j):
        rows = span(j)
        grad = normalize_back(t1[rows], gains[0:1], g2[rows] + total.get(j))
        g1[rows] = grad
        back.put(j, grad.astype(BF16))

    def heads_back(j):
        back.wait(j)
        made = mm_nt(back.both(j), mixing[...]).astype(BF16)
        da[place.core, span(j)] = made[:SEGMENT]
        da[place.other, span(j)] = made[SEGMENT:]

    pipeline(n, [(0, start), (1, total.middle), (3, finish), (4, heads_back)])
    each(n, total.drain, back.drain)


def key_rows(place, halo, j, scratch, own, from_before, from_after):
    for hh in range(2):
        scratch[hh] = halo.gathered(j, hh, own, from_before, from_after).astype(BF16)
    return [
        jnp.concatenate([scratch[place.core, i], scratch[place.other, i]], axis=0) for i in range(2)
    ]


def encoder_back_kernel(
    n_seq, halo_rows, dkv, dbefore, dafter, wkv, e3, e1, gains, hidden, inner_slope, side, side_slope,
    w1, w2, wd, wu, mixing,
    g1, da, down_grad, up_grad,
    from_before, from_after, rounded, g2, low_g2, low_g1,
    f0, f1, f2, f3, f4, b0, b1, b2, b3, b4, send, receive,
):
    place, sems = Place(n_seq), Sems(send, receive)
    half = e1.shape[0]
    n = half // SEGMENT
    halo = Halo(place, sems, 2 * half, halo_rows)
    first = Total(place, sems, (f0, f1, f2, f3, f4))
    back2 = Twins(place, sems, low_g2)
    second = Total(place, sems, (b0, b1, b2, b3, b4))
    back1 = Twins(place, sems, low_g1)
    place.greet([place.twin, place.across, place.before, place.after])

    def leave(j):
        for copy in halo.back_copies(j, dbefore, dafter, from_before, from_after):
            copy.start()

    each(n, leave)
    down_grad[...] = jnp.zeros_like(down_grad)
    up_grad[...] = jnp.zeros_like(up_grad)

    def start(j):
        for copy in halo.back_copies(j, dbefore, dafter, from_before, from_after):
            copy.wait_recv()
        key_grad, value_grad = key_rows(place, halo, j, rounded, dkv, from_before, from_after)
        first.put(j, mm_nt(key_grad, wkv[0]) + mm_nt(value_grad, wkv[1]))

    def turn(j):
        rows = span(j)
        grad = normalize_back(e3[rows], gains[1:2], first.get(j))
        g2[rows] = grad
        back2.put(j, grad.astype(BF16))

    def feed_back(j):
        back2.wait(j)
        rows = jnp.concatenate([hidden[place.core, span(j)], hidden[place.other, span(j)]], axis=0)
        piece, down, up = feed_rows_back(
            back2.both(j), rows, inner_slope[j], side[j], side_slope[j], w1, w2, wd, wu
        )
        down_grad[...] += down
        up_grad[...] += up
        second.put(j, piece)

    def finish(j):
        rows = span(j)
        grad = normalize_back(e1[rows], gains[0:1], g2[rows] + second.get(j))
        g1[rows] = grad
        back1.put(j, grad.astype(BF16))

    def heads_back(j):
        back1.wait(j)
        made = mm_nt(back1.both(j), mixing[...]).astype(BF16)
        da[place.core, span(j)] = made[:SEGMENT]
        da[place.other, span(j)] = made[SEGMENT:]

    pipeline(
        n,
        [
            (1, first.middle),
            (5, second.middle),
            (0, start),
            (3, turn),
            (4, feed_back),
            (7, finish),
            (8, heads_back),
        ],
    )

    def left(j):
        for copy in halo.back_copies(j, dbefore, dafter, from_before, from_after):
            copy.wait_send()

    each(n, left, first.drain, back2.drain, second.drain, back1.drain)


def input_back_kernel(
    n_seq, halo_rows, dq, dkv, dbefore, dafter, weights, g1,
    gradient, from_before, from_after, rounded, s0, s1, s2, s3, s4, send, receive,
):
    place, sems = Place(n_seq), Sems(send, receive)
    half = g1.shape[0]
    n = half // SEGMENT
    halo = Halo(place, sems, 2 * half, halo_rows)
    total = Total(place, sems, (s0, s1, s2, s3, s4))
    result = Twins(place, sems, gradient)
    place.greet([place.twin, place.across, place.before, place.after])

    def leave(j):
        for copy in halo.back_copies(j, dbefore, dafter, from_before, from_after):
            copy.start()

    each(n, leave)

    def start(j):
        for copy in halo.back_copies(j, dbefore, dafter, from_before, from_after):
            copy.wait_recv()
        key_grad, value_grad = key_rows(place, halo, j, rounded, dkv, from_before, from_after)
        query_grad = jnp.concatenate([dq[place.core, span(j)], dq[place.other, span(j)]], axis=0)
        total.put(
            j, mm_nt(query_grad, weights[0]) + mm_nt(key_grad, weights[1]) + mm_nt(value_grad, weights[2])
        )

    def finish(j):
        result.put(j, g1[span(j)] + total.get(j))

    pipeline(n, [(1, total.middle), (0, start), (3, finish)])

    def left(j):
        for copy in halo.back_copies(j, dbefore, dafter, from_before, from_after):
            copy.wait_send()

    each(n, left, total.drain, result.drain, result.wait)


def document_plan(query_docs, key_docs, query_rows, key_rows_, halo, block, causal):
    s = lax.axis_index("seq")
    own = lax.dynamic_slice_in_dim(query_docs, s * query_rows, query_rows)
    filler = jnp.full((halo,), -1, jnp.int32)
    padded = jnp.concatenate([filler, key_docs, filler])
    window = key_rows_ + 2 * halo
    keys = lax.dynamic_slice_in_dim(padded, s * key_rows_, window)
    blocks = own.reshape(-1, block)
    top = jnp.max(blocks, axis=1)
    bottom = jnp.min(jnp.where(blocks >= 0, blocks, 2**30), axis=1)
    read = (keys[None] >= bottom[:, None]) & (keys[None] <= top[:, None])
    index = jnp.arange(window, dtype=jnp.int32)[None]
    lo = jnp.min(jnp.where(read, index, window), axis=1) // KEY_BLOCK
    hi = (jnp.max(jnp.where(read, index + 1, 0), axis=1) + KEY_BLOCK - 1) // KEY_BLOCK
    if causal:
        ends = halo + block * (1 + jnp.arange(blocks.shape[0], dtype=jnp.int32))
        hi = jnp.minimum(hi, (ends + KEY_BLOCK - 1) // KEY_BLOCK)
    rows = jnp.where(blocks >= 0, blocks, -2)[:, None, :]
    return rows, keys[:, None], lo, hi


def halo_parts(kv, halo):
    size = lax.axis_size("seq")
    rows = kv.shape[1]
    up = [(i, i + 1) for i in range(size - 1)]
    down = [(i + 1, i) for i in range(size - 1)]
    before = lax.ppermute(kv[:, rows - halo :], "seq", up)
    after = lax.ppermute(kv[:, :halo], "seq", down)
    return before, kv, after


def halves(array):
    return array.reshape((2, array.shape[0] // 2) + array.shape[1:])


def exchange_scratch(half, *kinds):
    shapes = []
    for kind in kinds:
        if kind == "total":
            shapes += Total.SHAPES(half)
        else:
            shape, dtype = kind
            shapes.append(pltpu.VMEM(shape, dtype))
    return shapes


def on_device(
    n_seq,
    wide,
    source,
    target,
    source_document,
    target_document,
    cotangent,
    encoder_attention,
    encoder_mixing,
    encoder_gains,
    encoder_inner,
    encoder_outer,
    encoder_prefix,
    encoder_down,
    encoder_up,
    decoder_attention,
    decoder_mixing,
    decoder_prefix,
    cross_query,
    cross_memory,
    cross_mixing,
    cross_prefix,
    decoder_gains,
    decoder_inner,
    decoder_outer,
    decoder_down,
    decoder_up,
):
    ids = iter(range(1 + 16 * int(wide), 100))
    source_rows, width = source.shape
    target_rows = target.shape[0]
    cols = encoder_mixing.shape[0]
    hidden = encoder_inner.shape[1]
    adapt = encoder_down.shape[1]
    source_halo = source_rows if wide else source_rows // 2
    target_halo = target_rows if wide else target_rows // 2
    source_half, target_half = source_rows // 2, target_rows // 2
    source_n, target_n = source_half // SEGMENT, target_half // SEGMENT
    chunk = 2 * SEGMENT

    encoder_wo = lax.all_gather(encoder_mixing, "tp")
    decoder_wo = lax.all_gather(decoder_mixing, "tp")
    cross_wo = lax.all_gather(cross_mixing, "tp")

    def padded(prefix):
        return jnp.pad(prefix, ((0, 0), (0, PREFIX_ROWS - prefix.shape[1]), (0, 0)))

    encoder_prefix, decoder_prefix, cross_prefix = map(padded, (encoder_prefix, decoder_prefix, cross_prefix))

    encoder_q, encoder_kv = project(source, encoder_attention)
    encoder_parts = halo_parts(encoder_kv, source_halo)
    decoder_q, decoder_kv = project(target, decoder_attention)
    decoder_parts = halo_parts(decoder_kv, target_halo)

    encoder_docs = document_plan(
        source_document, source_document, source_rows, source_rows, source_halo, 256, False
    )
    decoder_docs = document_plan(
        target_document, target_document, target_rows, target_rows, target_halo, 128, True
    )
    cross_docs = document_plan(
        target_document, source_document, target_rows, source_rows, source_halo, 128, False
    )
    own_target = lax.dynamic_slice_in_dim(target_document, lax.axis_index("seq") * target_rows, target_rows)
    real = halves((own_target >= 0).astype(F32)[:, None])

    decoder_wide, decoder_low, decoder_total = attend(
        decoder_q, decoder_parts, decoder_prefix, decoder_docs, True
    )
    t1, t2, cross_q = exchange_call(
        partial(decoder_self_kernel, n_seq),
        next(ids),
        [((target_half, width), F32), ((target_half, width), F32), ((2, target_half, cols), BF16)],
        exchange_scratch(target_half, ((4, target_half, cols), BF16), ((2, target_half, width), BF16)),
        4,
        target_n,
        4 * target_rows * width * cols,
        (halves(decoder_low), halves(target), decoder_gains, decoder_wo, cross_query),
    )
    encoder_wide, encoder_low, encoder_total = attend(
        encoder_q, encoder_parts, encoder_prefix, encoder_docs, False
    )
    e1, e3, encoder_hidden, encoder_slope, encoder_side, encoder_side_slope, cross_kv, cross_before, cross_after = (
        exchange_call(
            partial(encoder_forward_kernel, n_seq, source_halo),
            next(ids),
            [
                ((source_half, width), F32),
                ((source_half, width), F32),
                ((2, source_half, width), BF16),
                ((source_n, chunk, hidden), BF16),
                ((source_n, chunk, adapt), BF16),
                ((source_n, chunk, adapt), BF16),
                ((2, source_rows, cols), BF16),
                ((2, source_halo, cols), BF16),
                ((2, source_halo, cols), BF16),
            ],
            exchange_scratch(
                source_half,
                ((4, source_half, cols), BF16),
                ((source_half, width), F32),
                "total",
                ((2, source_half, width), BF16),
            ),
            3 + 1 + 2 + 1 + (4 if wide else 2),
            source_n,
            2 * source_rows * width * (2 * hidden + 2 * adapt + 4 * cols),
            (
                halves(encoder_low), halves(source), encoder_gains, encoder_wo, encoder_inner, encoder_outer,
                encoder_down, encoder_up, cross_memory,
            ),
        )
    )
    cross_parts = (cross_before, cross_kv, cross_after)
    cross_q = cross_q.reshape(target_rows, cols)
    cross_wide, cross_low, cross_total = attend(cross_q, cross_parts, cross_prefix, cross_docs, False)

    decoded, g2, cross_da, decoder_down_gradient, decoder_up_gradient = exchange_call(
        partial(decoder_chain_kernel, n_seq),
        next(ids),
        [
            ((2, target_half, width), F32),
            ((target_half, width), F32),
            ((2, target_half, cols), BF16),
            ((width, adapt), F32),
            ((adapt, width), F32),
        ],
        exchange_scratch(
            target_half,
            ((4, target_half, cols), BF16),
            ((target_half, width), F32),
            ((target_half, width), F32),
            ((target_half, width), F32),
            ((2, target_half, width), BF16),
            ((2, target_half, width), BF16),
            ((2, target_half, width), BF16),
            ((target_n, chunk, hidden), BF16),
            ((target_n, chunk, adapt), BF16),
            ((target_n, chunk, adapt), BF16),
            "total",
            "total",
        ),
        3 + 1 + 2 + 1 + 1 + 2 + 1,
        target_n,
        2 * target_rows * width * (4 * hidden + 6 * adapt + 2 * cols),
        (
            halves(cross_low), t2, real, halves(cotangent), decoder_gains, cross_wo, decoder_inner,
            decoder_outer, decoder_down, decoder_up, cross_mixing,
        ),
    )

    cross_dq, cross_dbefore, cross_dkv, cross_dafter, cross_prefix_gradient = attend_back(
        cross_q, cross_da.reshape(target_rows, cols), cross_wide, cross_total, cross_parts, cross_prefix,
        cross_docs, False,
    )
    decoder_g1, decoder_da = exchange_call(
        partial(decoder_query_back_kernel, n_seq),
        next(ids),
        [((target_half, width), F32), ((2, target_half, cols), BF16)],
        exchange_scratch(target_half, ((2, target_half, width), BF16), "total"),
        3,
        target_n,
        4 * target_rows * width * cols,
        (halves(cross_dq), g2, t1, decoder_gains, cross_query, decoder_mixing),
    )
    encoder_g1, encoder_da, encoder_down_gradient, encoder_up_gradient = exchange_call(
        partial(encoder_back_kernel, n_seq, source_halo),
        next(ids),
        [
            ((source_half, width), F32),
            ((2, source_half, cols), BF16),
            ((width, adapt), F32),
            ((adapt, width), F32),
        ],
        exchange_scratch(
            source_half,
            ((2, source_halo, cols), BF16),
            ((2, source_halo, cols), BF16),
            ((2, 2, SEGMENT, cols), BF16),
            ((source_half, width), F32),
            ((2, source_half, width), BF16),
            ((2, source_half, width), BF16),
            "total",
            "total",
        ),
        (4 if wide else 2) + 2 + 1 + 2 + 1,
        source_n,
        2 * source_rows * width * (2 * hidden + 4 * adapt + 3 * cols),
        (
            cross_dkv, cross_dbefore, cross_dafter, cross_memory, e3, e1, encoder_gains, encoder_hidden,
            encoder_slope, encoder_side, encoder_side_slope, encoder_inner, encoder_outer, encoder_down,
            encoder_up, encoder_mixing,
        ),
    )

    def input_back(dq, dkv, dbefore, dafter, weights, g1, rows, halo):
        half = rows // 2
        return exchange_call(
            partial(input_back_kernel, n_seq, halo),
            next(ids),
            [((2, half, width), F32)],
            exchange_scratch(
                half,
                ((2, halo, cols), BF16),
                ((2, halo, cols), BF16),
                ((2, 2, SEGMENT, cols), BF16),
                "total",
            ),
            (4 if wide else 2) + 2 + 1,
            half // SEGMENT,
            6 * rows * width * cols,
            (halves(dq), dkv, dbefore, dafter, weights, g1),
        )[0].reshape(rows, width)

    dq, dbefore, dkv, dafter, decoder_prefix_gradient = attend_back(
        decoder_q, decoder_da.reshape(target_rows, cols), decoder_wide, decoder_total, decoder_parts,
        decoder_prefix, decoder_docs, True,
    )
    target_gradient = input_back(
        dq, dkv, dbefore, dafter, decoder_attention, decoder_g1, target_rows, target_halo
    )
    dq, dbefore, dkv, dafter, encoder_prefix_gradient = attend_back(
        encoder_q, encoder_da.reshape(source_rows, cols), encoder_wide, encoder_total, encoder_parts,
        encoder_prefix, encoder_docs, False,
    )
    source_gradient = input_back(
        dq, dkv, dbefore, dafter, encoder_attention, encoder_g1, source_rows, source_halo
    )

    cut = slice(0, PREFIX)
    weight_totals = lax.psum(
        (
            encoder_prefix_gradient[:, cut],
            encoder_down_gradient,
            encoder_up_gradient,
            decoder_prefix_gradient[:, cut],
            cross_prefix_gradient[:, cut],
            decoder_down_gradient,
            decoder_up_gradient,
        ),
        "seq",
    )
    return (decoded.reshape(target_rows, width), source_gradient, target_gradient) + tuple(weight_totals)


def solution(mesh):
    return jax.shard_map(
        partial(on_device, mesh.shape["seq"], True),
        mesh=mesh,
        in_specs=(
            P("seq", None),
            P("seq", None),
            P(),
            P(),
            P("seq", None),
            P(None, None, "tp"),
            P("tp", None),
            P(),
            P(None, "tp"),
            P("tp", None),
            P(None, None, "tp"),
            P(None, "tp"),
            P("tp", None),
            P(None, None, "tp"),
            P("tp", None),
            P(None, None, "tp"),
            P(None, "tp"),
            P(None, None, "tp"),
            P("tp", None),
            P(None, None, "tp"),
            P(),
            P(None, "tp"),
            P("tp", None),
            P(None, "tp"),
            P("tp", None),
        ),
        out_specs=(
            P("seq", None),
            P("seq", None),
            P("seq", None),
            P(None, None, "tp"),
            P(None, "tp"),
            P("tp", None),
            P(None, None, "tp"),
            P(None, None, "tp"),
            P(None, "tp"),
            P("tp", None),
        ),
        check_vma=False,
    )
```

time: 1700 us -> 646 us (0.38)
  waiting for transfers between devices: 1030 us -> 141 us
  Pallas kernels: 0 us -> 449 us
  matrix products: 399 us -> 0 us
  other arithmetic: 127 us -> 3.84 us
  local copies, waits for them, and re-layouts: 78.3 us -> 22.6 us
  starting transfers between devices: 38.4 us -> 13.6 us
    psum x10 -> x2, waiting for transfers between devices: 741 us -> 103 us  [on_device(): lax.psum((encoder_prefix_gradient[:, cut], encoder_down_gradient, encoder...]
    pallas_call x0 -> x15, Pallas kernels: none -> 449 us  [the longest x7 364 us: exchange_call(): pl.pallas_call(kernel, in_specs=[vmem] * len(args), out_specs=[vmem] * le...]
    dot_general x94 -> x0, matrix products: 399 us -> none  [the longest x6 65.7 us: window_scores(): jnp.einsum('qhd,khd->hqk', queries, key_heads, preferred_element_type=jnp...]
    ppermute x12 -> x4, waiting for transfers between devices: 288 us -> 36.2 us  [the longest x2 36.2 us: halo_parts(): before = lax.ppermute(kv[:, rows - halo:], 'seq', up)]
    reduce_sum x29 -> x0, other arithmetic: 83.9 us -> none  [the longest x4 42.9 us: forward_block(): jnp.sum(jnp.exp(main - highest[:, :, None]), axis=2)]
    ppermute x12 -> x4, starting transfers between devices: 37.3 us -> 13.4 us  [the longest x2 10.7 us: halo_parts(): before = lax.ppermute(kv[:, rows - halo:], 'seq', up)]
    slice x14 -> x0, local copies, waits for them, and re-layouts: 21 us -> none  [the longest x6 12.5 us: attend(): value_heads = as_heads(window[:, 1])]
    unnamed x314 -> x45, local copies, waits for them, and re-layouts: 37.4 us -> 17 us
  transfers between devices with their start and end apart: 22 -> 9, of which waited for: 14 -> 4; matrix products, arithmetic and copies ran while one was open for 6% -> 2% of each run, Pallas kernels for 0% -> 38%
where the time goes in v1:
time: 646 us; the launch traced here: 644 us
  Pallas kernels  449 us (70%)
  waiting for transfers between devices  141 us (22%)
  local copies, waits for them, and re-layouts  22.6 us (3%)
  between operations  14.1 us (2%)
  starting transfers between devices  13.6 us (2%)
    pallas_call x7, Pallas kernels, exchange_call(): pl.pallas_call(kernel, in_specs=[vmem] * len(args), out_specs=[vmem] * le...  364 us
    psum x2, waiting for transfers between devices, on_device(): lax.psum((encoder_prefix_gradient[:, cut], encoder_down_gradient, encoder...  103 us
    pallas_call x3, Pallas kernels, attend_back(): pl.pallas_call(partial(attend_back_kernel, halo, causal), grid_spec=pltpu...  42.8 us
    ppermute x2, waiting for transfers between devices, halo_parts(): before = lax.ppermute(kv[:, rows - halo:], 'seq', up)  36.2 us
    pallas_call x3, Pallas kernels, attend(): pl.pallas_call(partial(attend_kernel, halo, causal), grid_spec=pltpu.Pref...  32.9 us
    unnamed x45, local copies, waits for them, and re-layouts  17 us
  transfers between devices with their start and end apart: 9, of which 4 were waited for; matrix products, arithmetic and copies ran while one was open for 2% of the time, Pallas kernels for 38%

profile of v1, /device:TPU:0, one launch (start us, length us, event | category | flops | bytes accessed | tf_op | source)
XLA Modules:
  0.0 644.0 jit_solution(4217956368041653993)
XLA Ops:
  8.7 3.5 shard_map.312
  12.2 1.4 collective-permute-start.1
  13.7 5.5 collective-permute-start
  19.2 5.6 shard_map.315
  24.7 1.3 collective-permute-start.3
  26.0 5.2 collective-permute-start.2
  34.1 1.2 broadcast_in_dim.112.kd_ref
  38.1 1.7 copy.57.kd_ref
  40.9 22.5 %collective-permute-done.bef_ref = bf16[2,512,256]{2,1,0:T(8,128)(2,1)S(1)} collective-permute-done((bf16[2,512,256]{2,1,0:T(8,128)(2,1)}, bf16[2,512,256]{2,1,0:T(8,128)(2,1)S(1)}, u32[]{:S(2)}, u32[]{:S(2)}) %collective-permute-start) | collective-permute-done | bytes 524320 | tf_op jit(solution)/shard_map/ppermute | solution.py:960
  64.2 7.9 %shard_map.313 = (f32[512,256]{1,0:T(8,128)}, bf16[512,256]{1,0:T(8,128)(2,1)}, f32[4,1,512]{2,1,0:T(1,128)}) custom-call(s32[4]{0:T(128)} %get-tuple-element.167.lo_ref, s32[4]{0:T(128)} %get-tuple-element.168.hi_ref, bf16[512,256]{1,0:T(8,128)(2,1)} %get-tuple-element.61.q_ref, bf16[2,512,256]{2,1,0:T(8,128)(2,1)} %copy-done.15, ...), custom_call_target="tpu_custom_call" | custom-call | flops 2147483648 | bytes 3145728 | tf_op jit(solution)/shard_map/pallas_call | solution.py:187
  72.1 13.7 %collective-permute-done.2.bef_ref = bf16[2,1024,256]{2,1,0:T(8,128)(2,1)S(1)} collective-permute-done((bf16[2,1024,256]{2,1,0:T(8,128)(2,1)}, bf16[2,1024,256]{2,1,0:T(8,128)(2,1)S(1)}, u32[]{:S(2)}, u32[]{:S(2)}) %collective-permute-start.2) | collective-permute-done | bytes 1048608 | tf_op jit(solution)/shard_map/ppermute | solution.py:960
  85.8 1.0 copy-done.13
  86.8 13.5 %shard_map.316 = (f32[1024,256]{1,0:T(8,128)}, bf16[1024,256]{1,0:T(8,128)(2,1)}, f32[4,1,1024]{2,1,0:T(1,128)}) custom-call(s32[4]{0:T(128)} %get-tuple-element.164.lo_ref, s32[4]{0:T(128)} %get-tuple-element.163.hi_ref, bf16[1024,256]{1,0:T(8,128)(2,1)} %get-tuple-element.65.q_ref, bf16[2,1024,256]{2,1,0:T(8,128)(2,1)} %copy-done.13, ...), custom_call_target="tpu_custom_call" | custom-call | flops 4294967296 | bytes 6291456 | tf_op jit(solution)/shard_map/pallas_call | solution.py:187
  100.3 14.3 %shard_map.314 = (f32[256,1024]{1,0:T(8,128)}, f32[256,1024]{1,0:T(8,128)}, bf16[2,256,256]{2,1,0:T(8,128)(2,1)}) custom-call(bf16[2,256,256]{2,1,0:T(8,128)(2,1)} %bitcast.36, bf16[2,256,1024]{2,1,0:T(8,128)(2,1)} %bitcast.32, f32[3,1024]{1,0:T(4,128)} %gains.9, bf16[4,256,1024]{2,1,0:T(8,128)(2,1)} %bitcast.31, bf16[1024,256]{1,0:T(8,128)(2,1)} %wq.3), custom_call_target="tpu_custom_call" | custom-call | flops 536870912 | bytes 3944448 | tf_op jit(solution)/shard_map/pallas_call | solution.py:579
  114.6 81.1 %shard_map.317 = (f32[512,1024]{1,0:T(8,128)}, f32[512,1024]{1,0:T(8,128)}, bf16[2,512,1024]{2,1,0:T(8,128)(2,1)}, bf16[8,128,1024]{2,1,0:T(8,128)(2,1)}, bf16[8...) custom-call(bf16[2,512,256]{2,1,0:T(8,128)(2,1)} %bitcast.51, ...), custom_call_target="tpu_custom_call" | custom-call | flops 6979321856 | bytes 10493952 | tf_op jit(solution)/shard_map/pallas_call | solution.py:579
  195.7 11.5 %shard_map.318 = (f32[512,256]{1,0:T(8,128)}, bf16[512,256]{1,0:T(8,128)(2,1)}, f32[4,1,512]{2,1,0:T(1,128)}) custom-call(s32[4]{0:T(128)} %get-tuple-element.166.lo_ref, s32[4]{0:T(128)} %get-tuple-element.165.hi_ref, bf16[512,256]{1,0:T(8,128)(2,1)} %bitcast.47, bf16[2,1024,256]{2,1,0:T(8,128)(2,1)} %get-tuple-element.68.bef_ref, ...), custom_call_target="tpu_custom_call" | custom-call | flops 2147483648 | bytes 6291456 | tf_op jit(solution)/shard_map/pallas_call | solution.py:187
  207.2 46.5 %shard_map.319 = (f32[2,256,1024]{2,1,0:T(8,128)}, f32[256,1024]{1,0:T(8,128)}, bf16[2,256,256]{2,1,0:T(8,128)(2,1)}, f32[1024,128]{1,0:T(8,128)}, f32[128,1024]{1,0:T(8,128)}) custom-call(bf16[2,256,256]{2,1,0:T(8,128)(2,1)} %bitcast.53, f32[256,1024]{1,0:T(8,128)} %get-tuple-element.72.t2, f32[2,256,1]{2,1,0:T(8,128)} %reshape.157.real, ...), custom_call_target="tpu_custom_call" | custom-call | flops 5637144576 | bytes 9713664 | tf_op jit(solution)/shard_map/pallas_call | solution.py:579
  253.8 15.0 %shard_map.320 = (bf16[512,256]{1,0:T(8,128)(2,1)}, bf16[2,1024,256]{2,1,0:T(8,128)(2,1)}, f32[2,1024,256]{2,1,0:T(8,128)}, bf16[2,1024,256]{2,1,0:T(8,128)(2,1)}, f32[2,32,256]{2,1,0:T(8,128)}) custom-call(s32[4]{0:T(128)} %get-tuple-element.166.lo_ref, s32[4]{0:T(128)} %get-tuple-element.165.hi_ref, bf16[512,256]{1,0:T(8,128)(2,1)} %bitcast.48, ...), custom_call_target="tpu_custom_call" | custom-call | flops 5368709120 | bytes 12582912 | tf_op jit(solution)/shard_map/pallas_call | solution.py:308
  268.8 20.4 %shard_map.324 = (f32[256,1024]{1,0:T(8,128)}, bf16[2,256,256]{2,1,0:T(8,128)(2,1)}) custom-call(bf16[2,256,256]{2,1,0:T(8,128)(2,1)} %bitcast.35, f32[256,1024]{1,0:T(8,128)} %get-tuple-element.95.g2, f32[256,1024]{1,0:T(8,128)} %get-tuple-element.96.t1, f32[3,1024]{1,0:T(4,128)} %gains.9, bf16[1024,256]{1,0:T(8,128)(2,1)} %wq.3, bf16[256,1024]{1,0:T(8,128)(2,1)} %mixing.5), custom_call_target="tpu_custom_call" | custom-call | flops 536870912 | bytes 3420160 | tf_op jit(solution)/shard_map/pallas_call | solution.py:579
  289.1 94.0 %shard_map.321 = (f32[512,1024]{1,0:T(8,128)}, bf16[2,512,256]{2,1,0:T(8,128)(2,1)}, f32[1024,128]{1,0:T(8,128)}, f32[128,1024]{1,0:T(8,128)}) custom-call(f32[2,1024,256]{2,1,0:T(8,128)} %get-tuple-element.77.dkv, bf16[2,1024,256]{2,1,0:T(8,128)(2,1)} %get-tuple-element.78.dbefore, bf16[2,1024,256]{2,1,0:T(8,128)(2,1)} %get-tuple-element.79.dafter, ...), custom_call_target="tpu_custom_call" | custom-call | flops 6979321856 | bytes 19406848 | tf_op jit(solution)/shard_map/pallas_call | solution.py:579
  383.2 9.8 %shard_map.325 = (bf16[512,256]{1,0:T(8,128)(2,1)}, bf16[2,512,256]{2,1,0:T(8,128)(2,1)}, f32[2,512,256]{2,1,0:T(8,128)}, bf16[2,512,256]{2,1,0:T(8,128)(2,1)}, f32[2,32,256]{2,1,0:T(8,128)}) custom-call(s32[4]{0:T(128)} %get-tuple-element.167.lo_ref, s32[4]{0:T(128)} %get-tuple-element.168.hi_ref, bf16[512,256]{1,0:T(8,128)(2,1)} %get-tuple-element.61.q_ref, ...), custom_call_target="tpu_custom_call" | custom-call | flops 5368709120 | bytes 6291456 | tf_op jit(solution)/shard_map/pallas_call | solution.py:308
  392.9 18.1 %shard_map.322 = (bf16[1024,256]{1,0:T(8,128)(2,1)}, bf16[2,1024,256]{2,1,0:T(8,128)(2,1)}, f32[2,1024,256]{2,1,0:T(8,128)}, bf16[2,1024,256]{2,1,0:T(8,128)(2,1)}, f32[2,32,256]{2,1,0:T(8,128)}) custom-call(s32[4]{0:T(128)} %get-tuple-element.164.lo_ref, s32[4]{0:T(128)} %get-tuple-element.163.hi_ref, bf16[1024,256]{1,0:T(8,128)(2,1)} %get-tuple-element.65.q_ref, ...), custom_call_target="tpu_custom_call" | custom-call | flops 10737418240 | bytes 12582912 | tf_op jit(solution)/shard_map/pallas_call | solution.py:308
  411.6 44.6 %shard_map.326 = f32[2,256,1024]{2,1,0:T(8,128)} custom-call(bf16[2,256,256]{2,1,0:T(8,128)(2,1)} %bitcast.34, f32[2,512,256]{2,1,0:T(8,128)} %get-tuple-element.101.dkv, bf16[2,512,256]{2,1,0:T(8,128)(2,1)} %get-tuple-element.102.dbefore, bf16[2,512,256]{2,1,0:T(8,128)(2,1)} %get-tuple-element.103.dafter, bf16[3,1024,256]{2,1,0:T(8,128)(2,1)} %weights.3, ...), custom_call_target="tpu_custom_call" | custom-call | flops 805306368 | bytes 4980736 | tf_op jit(solution)/shard_map/pallas_call | solution.py:579
  456.2 63.1 %shard_map.323 = f32[2,512,1024]{2,1,0:T(8,128)} custom-call(bf16[2,512,256]{2,1,0:T(8,128)(2,1)} %bitcast.33, f32[2,1024,256]{2,1,0:T(8,128)} %get-tuple-element.90.dkv, bf16[2,1024,256]{2,1,0:T(8,128)(2,1)} %get-tuple-element.91.dbefore, bf16[2,1024,256]{2,1,0:T(8,128)(2,1)} %get-tuple-element.92.dafter, bf16[3,1024,256]{2,1,0:T(8,128)(2,1)} %weights.2, ...), custom_call_target="tpu_custom_call" | custom-call | flops 1610612736 | bytes 8388608 | tf_op jit(solution)/shard_map/pallas_call | solution.py:579
  519.7 1.5 copy.64
  521.2 1.5 copy.65
  522.7 1.5 copy.66
  524.2 102.7 %all-reduce.10.cloned.1.call-done = (f32[1024,128]{1,0:T(8,128)}, f32[128,1024]{1,0:T(8,128)}, f32[1024,128]{1,0:T(8,128)}, f32[128,1024]{1,0:T(8,128)}) async-done(((f32[1024,128]{1,0:T(8,128)}, f32[128,1024]{1,0:T(8,128)}, f32[1024,128]{1,0:T(8,128)}, f32[128,1024]{1,0:T(8,128)}), (f32[1024,128]{1,0:T(8,128)}, f32[128,1024]{1,0:T(8,128)}, f32[1024,128]{1,0:T(8,128)}, ...) | async-done | bytes 2097168 | tf_op jit(solution)/shard_map/psum | solution.py:1211
  626.8 1.3 copy.81
  628.2 1.6 copy-done
  629.8 2.1 copy.82
  632.9 1.3 copy.83
  (76 shorter events, 14.2 us)
Async XLA Ops:
  7.2 93.1 %all-gather.7.cloned.1.call-start = ((), (), s32[]{:S(2)}) async-start(), calls=%async_computation | async-start | bytes 2621440 | tf_op jit(solution)/shard_map/all_gather | solution.py:1022
  7.9 106.7 %all-gather.9.cloned.1.call-start = ((), (), s32[]{:S(2)}) async-start(), calls=%async_computation.1 | async-start | bytes 2621440 | tf_op jit(solution)/shard_map/all_gather | solution.py:1021
  8.7 198.6 %all-gather.11.cloned.1.call-start = ((), (), s32[]{:S(2)}) async-start(), calls=%async_computation.2 | async-start | bytes 2621440 | tf_op jit(solution)/shard_map/all_gather | solution.py:1023
  12.2 19.1 %copy-start.11 = (s32[4096]{0:T(1024)S(1)}, s32[4096]{0:T(1024)}, u32[]{:S(2)}) copy-start(s32[4096]{0:T(1024)} %param.28) | copy-start | bytes 49156
  12.2 19.3 %copy-start.7 = (s32[8192]{0:T(1024)S(1)}, s32[8192]{0:T(1024)}, u32[]{:S(2)}) copy-start(s32[8192]{0:T(1024)} %param.27) | copy-start | bytes 98308
  12.2 23.1 %copy-start.8 = (bf16[2,30,256]{2,0,1:T(2,128)(2,1)S(1)}, bf16[2,30,256]{2,0,1:T(2,128)(2,1)}, u32[]{:S(2)}) copy-start(bf16[2,30,256]{2,0,1:T(2,128)(2,1)} %param.35) | copy-start | bytes 92164
  12.2 23.1 %copy-start.9 = (bf16[2,30,256]{2,0,1:T(2,128)(2,1)S(1)}, bf16[2,30,256]{2,0,1:T(2,128)(2,1)}, u32[]{:S(2)}) copy-start(bf16[2,30,256]{2,0,1:T(2,128)(2,1)} %param.40) | copy-start | bytes 92164
  12.2 24.3 %copy-start.10 = (bf16[2,30,256]{2,0,1:T(2,128)(2,1)S(1)}, bf16[2,30,256]{2,0,1:T(2,128)(2,1)}, u32[]{:S(2)}) copy-start(bf16[2,30,256]{2,0,1:T(2,128)(2,1)} %param.44) | copy-start | bytes 92164
  12.2 28.6 %collective-permute-start.1 = (bf16[2,512,256]{2,1,0:T(8,128)(2,1)}, bf16[2,512,256]{2,1,0:T(8,128)(2,1)S(1)}, u32[]{:S(2)}, u32[]{:S(2)}) collective-permute-start(bf16[2,512,256]{2,1,0:T(8,128)(2,1)} %get-tuple-element.62.own_ref), channel_id=1, source_target_pairs={{4,0},{8,4},{12,8},{16,12},{20,16},{24,20},{28,24},{5,1},{9,5},{13... | collective-permute-start | bytes 1572872 | tf_op jit(solution)/shard_map/ppermute | solution.py:961
  13.7 49.7 %collective-permute-start = (bf16[2,512,256]{2,1,0:T(8,128)(2,1)}, bf16[2,512,256]{2,1,0:T(8,128)(2,1)S(1)}, u32[]{:S(2)}, u32[]{:S(2)}) collective-permute-start(bf16[2,512,256]{2,1,0:T(8,128)(2,1)} %get-tuple-element.62.own_ref), channel_id=1, source_target_pairs={{0,4},{4,8},{8,12},{12,16},{16,20},{20,24},{24,28},{1,5},{5,9},{9,... | collective-permute-start | bytes 1572872 | tf_op jit(solution)/shard_map/ppermute | solution.py:960
  24.7 47.3 %collective-permute-start.3 = (bf16[2,1024,256]{2,1,0:T(8,128)(2,1)}, bf16[2,1024,256]{2,1,0:T(8,128)(2,1)S(1)}, u32[]{:S(2)}, u32[]{:S(2)}) collective-permute-start(bf16[2,1024,256]{2,1,0:T(8,128)(2,1)} %get-tuple-element.66.own_ref), channel_id=1, source_target_pairs={{4,0},{8,4},{12,8},{16,12},{20,16},{24,20},{28,24},{5,1},{9,5},{13... | collective-permute-start | bytes 3145736 | tf_op jit(solution)/shard_map/ppermute | solution.py:961
  26.0 59.7 %collective-permute-start.2 = (bf16[2,1024,256]{2,1,0:T(8,128)(2,1)}, bf16[2,1024,256]{2,1,0:T(8,128)(2,1)S(1)}, u32[]{:S(2)}, u32[]{:S(2)}) collective-permute-start(bf16[2,1024,256]{2,1,0:T(8,128)(2,1)} %get-tuple-element.66.own_ref), channel_id=1, source_target_pairs={{0,4},{4,8},{8,12},{12,16},{16,20},{20,24},{24,28},{1,5},{5,9},{9,... | collective-permute-start | bytes 3145736 | tf_op jit(solution)/shard_map/ppermute | solution.py:960
  31.2 488.4 %all-reduce.8.cloned.1.call-start = ((), (), s32[]{:S(2)}) async-start(), calls=%async_computation.3 | async-start | bytes 393216 | tf_op jit(solution)/shard_map/psum | solution.py:1211
  40.9 22.5 %copy-start.14 = (bf16[2,512,256]{2,1,0:T(8,128)(2,1)}, bf16[2,512,256]{2,1,0:T(8,128)(2,1)S(1)}, u32[]{:S(2)}) copy-start(bf16[2,512,256]{2,1,0:T(8,128)(2,1)S(1)} %collective-permute-done.1.aft_ref) | copy-start | bytes 1572868
  63.4 0.8 copy-start.15
  72.1 13.7 %copy-start.12 = (bf16[2,1024,256]{2,1,0:T(8,128)(2,1)}, bf16[2,1024,256]{2,1,0:T(8,128)(2,1)S(1)}, u32[]{:S(2)}) copy-start(bf16[2,1024,256]{2,1,0:T(8,128)(2,1)S(1)} %collective-permute-done.3.aft_ref) | copy-start | bytes 3145732
  85.8 1.0 copy-start.13
  411.0 215.8 %all-reduce.10.cloned.1.call-start = ((), (), s32[]{:S(2)}) async-start(), calls=%async_computation.4 | async-start | bytes 4194304 | tf_op jit(solution)/shard_map/psum | solution.py:1211
  456.2 170.6 %copy-start.2 = (f32[2,256,1024]{2,1,0:T(8,128)S(1)}, f32[2,256,1024]{2,1,0:T(8,128)}, u32[]{:S(2)}) copy-start(f32[2,256,1024]{2,1,0:T(8,128)} %get-tuple-element.73) | copy-start | bytes 6291460
  626.8 2.9 copy-start
  629.8 3.1 copy-start.1
  632.9 1.4 copy-start.6
  632.9 2.2 copy-start.5
  634.3 1.6 copy-start.4
  634.3 2.4 copy-start.3
Sparse Core Ops, SparseCore 0:
  9.6 25.2 all-gather.6
  36.4 22.5 all-gather.8
  60.6 22.5 all-gather.10
  411.2 108.4 all-reduce.7
  524.0 102.7 all-reduce.9
